TPU v7x, 32 devices: a whole 2x2x4 slice. The times are simulated.
32 devices in a mesh: tile: 8 (over z, y), row: 2 (over core), col: 2 (over x).
Axes of the slice: x: 2, y: 2, z: 4, core: 2. Of those that a mesh axis runs over, the one named last changes fastest.
Arguments:
- tile_tokens: bfloat16 [96, 256, 1536], P(('tile', 'row', 'col')), may hold values from -6 to 6
- tile_count: int32 [32], replicated, may hold values from 1 to 3, as said below
- tile_cell: int32 [96], replicated, may hold values from 0 to 127, as said below
- occupancy: int32 [32, 4], replicated, may hold values from 0 to 1, as said below
- block_mask: int32 [16, 2, 8], P(('tile', 'row'), 'col'), may hold values 0 or 1
- enc_gain: float32 [1536], replicated, may hold values from 0.25 to 1.75
- w_query: bfloat16 [1536, 768], P('tile'), may hold values from -1 to 1
- w_key: bfloat16 [1536, 768], P('tile'), may hold values from -1 to 1
- w_value: bfloat16 [1536, 768], P('tile'), may hold values from -0.15625 to 0.15625
- w_out_t: bfloat16 [1536, 768], P('tile'), may hold values from -0.21875 to 0.21875
- final_gain: float32 [1536], replicated, may hold values from 0.25 to 1.75
- w_proj: bfloat16 [1536, 768], P('tile'), may hold values from -0.15625 to 0.15625
- slide_gain: float32 [768], replicated, may hold values from 0.25 to 1.75
- s_query: bfloat16 [768, 384], P('tile'), may hold values from -1 to 1
- s_key: bfloat16 [768, 384], P('tile'), may hold values from -1 to 1
- s_value: bfloat16 [768, 384], P('tile'), may hold values from -0.21875 to 0.21875
- s_out_t: bfloat16 [768, 384], P('tile'), may hold values from -0.3125 to 0.3125
Outputs:
- grid_tokens: bfloat16 [32, 4, 768], P(('tile', 'row'), 'col')
- slide_branch: float32 [32, 4, 768], P(('tile', 'row'), 'col')
Inputs may be any that keep to these rules, and one draw needn't show every extreme that they name: Only the first tile_count[d] slots of device d hold tissue tiles; some device holds exactly 3. `tile_cell`: A slot of the device with indices (t, r, c) lies in grid column block c and in a grid row block b * 2 + r for some b, blocks being 2 x 2 cells. No two slots share a cell. The slots of one device lie in distinct row blocks, and for each slot number the slots of the 8 devices (t, r, c) with fixed r and c lie in distinct row blocks. `occupancy`: 1 exactly at the cells of the live slots.
All inputs are finite; a program needn't handle non-finite values. No bound on the sum of `block_mask` on one device may be relied on, other than what follows from the above.
Results may differ from a plain program's by a relative error of at most 0.017.
Values may be sent and summed in bfloat16 or wider, within the bound.
A program may use at most 64 MiB of HBM per device.

v0:
```python
import math

import jax
import jax.numpy as jnp
from jax import lax
from jax.sharding import PartitionSpec as P

HD = 64
HDS = 48
BLOCK = 2


def with_halo(cells, sides, width):
    for axis, dim in sides:
        count = lax.axis_size(axis)
        ends = count - 1
        head = lax.slice_in_dim(cells, 0, width, axis=dim)
        tail = lax.slice_in_dim(cells, cells.shape[dim] - width, cells.shape[dim], axis=dim)
        cells = jnp.concatenate(
            [
                lax.ppermute(tail, axis, [(i, (i + 1) % count) for i in range(ends)]),
                cells,
                lax.ppermute(head, axis, [((i + 1) % count, i) for i in range(ends)]),
            ],
            axis=dim,
        )
    return cells


def layer_norm(vector, scale_gain, epsilon):
    row_mean = jnp.mean(vector, axis=-1, keepdims=True)
    centered = vector - row_mean
    spread = jnp.mean(centered * centered, axis=-1, keepdims=True)
    return centered * lax.rsqrt(spread + epsilon) * scale_gain


def contract_last(first_op, second_op):
    return lax.dot_general(
        first_op,
        second_op,
        (((first_op.ndim - 1,), (1,)), ((), ())),
        preferred_element_type=jnp.float32,
    )


def class_branch(one_tile, query_row, enc_gain, key_part, value_part):
    wide_tile = one_tile.astype(jnp.float32)
    normed = layer_norm(wide_tile, enc_gain, 1e-06).astype(jnp.bfloat16)
    tile_keys = jnp.dot(normed, key_part, preferred_element_type=jnp.float32).astype(jnp.bfloat16)
    tile_values = jnp.dot(normed, value_part, preferred_element_type=jnp.float32).astype(
        jnp.bfloat16
    )
    head_count = key_part.shape[1] // HD
    scores = jnp.einsum(
        "hd,phd->hp",
        query_row.reshape(head_count, HD),
        tile_keys.reshape(-1, head_count, HD),
        preferred_element_type=jnp.float32,
    ) / math.sqrt(HD)
    row_peak = jnp.max(scores, axis=1, keepdims=True)
    weights_exp = jnp.exp(scores - row_peak)
    soft = (weights_exp / jnp.sum(weights_exp, axis=1, keepdims=True)).astype(jnp.bfloat16)
    return (
        jnp.einsum(
            "hp,phd->hd",
            soft,
            tile_values.reshape(-1, head_count, HD),
            preferred_element_type=jnp.float32,
        )
        .reshape(1, -1)
        .astype(jnp.bfloat16)
    )


def partial_rows(buffer, queries, low_row, high_row, weights, out_part):
    enc_gain, key_part, value_part = weights
    row_width = out_part.shape[0]

    def one_slot(slot_index, running):
        one_tile = lax.dynamic_index_in_dim(buffer, slot_index, 0, keepdims=False)
        query_row = lax.dynamic_index_in_dim(queries, slot_index, 0, keepdims=False)
        class_mix = class_branch(one_tile, query_row, enc_gain, key_part, value_part)
        result_row = contract_last(class_mix, out_part)[0]
        return lax.dynamic_update_index_in_dim(running, result_row, slot_index, 0)

    blank_rows = jnp.zeros((buffer.shape[0], row_width), jnp.float32)
    return lax.fori_loop(low_row, high_row, one_slot, blank_rows)


def encode_segment(buffer, queries, low_row, high_row, weights, out_part, final_gain, w_proj):
    partial_value = partial_rows(buffer, queries, low_row, high_row, weights, out_part)
    carried = buffer[:, 0, :].astype(jnp.float32) + partial_value
    final_rows = layer_norm(carried, final_gain, 1e-06).astype(jnp.bfloat16)
    result = jnp.dot(final_rows, w_proj, preferred_element_type=jnp.float32).astype(jnp.bfloat16)
    slot_ids = jnp.arange(buffer.shape[0])
    kept = (slot_ids >= low_row) & (slot_ids < high_row)
    return jnp.where(kept[:, None], result, jnp.zeros_like(result))


def local(
    tile_tokens,
    tile_count,
    tile_cell,
    occupancy,
    block_mask,
    enc_gain,
    w_query,
    w_key,
    w_value,
    w_out_t,
    final_gain,
    w_proj,
    slide_gain,
    s_query,
    s_key,
    s_value,
    s_out_t,
):
    tile_devices = lax.axis_size("tile")
    row_devices = lax.axis_size("row")
    column_devices = lax.axis_size("col")
    tile_index = lax.axis_index("tile")
    row_index = lax.axis_index("row")
    column_index = lax.axis_index("col")
    slot_total = tile_tokens.shape[0]
    counts = tile_count.reshape(tile_devices, row_devices, column_devices)
    class_raw = tile_tokens[:, 0, :]
    key_value = (
        lax.all_gather(w_key, "tile", axis=0, tiled=True),
        lax.all_gather(w_value, "tile", axis=0, tiled=True),
    )
    weights = (enc_gain, key_value[0], key_value[1])
    class_side = (
        lax.all_gather(w_query, "tile", axis=0, tiled=True),
        lax.all_gather(w_out_t, "tile", axis=0, tiled=True),
        lax.all_gather(w_proj, "tile", axis=0, tiled=True),
    )
    own_normed = layer_norm(class_raw.astype(jnp.float32), enc_gain, 1e-06).astype(jnp.bfloat16)
    queries = jnp.dot(own_normed, class_side[0], preferred_element_type=jnp.float32).astype(
        jnp.bfloat16
    )
    out_part = class_side[1]
    full_proj = class_side[2]
    slide_full = (
        lax.all_gather(s_query, "tile", axis=0, tiled=True),
        lax.all_gather(s_key, "tile", axis=0, tiled=True),
        lax.all_gather(s_value, "tile", axis=0, tiled=True),
        lax.all_gather(s_out_t, "tile", axis=0, tiled=True),
    )
    own_count = counts[tile_index, row_index, column_index]
    encoded = encode_segment(
        tile_tokens, queries, 0, own_count, weights, out_part, final_gain, full_proj
    )
    width_model = encoded.shape[1]
    group_cells = tile_cell.reshape(tile_devices, row_devices, column_devices, slot_total)[
        :, row_index, column_index, :
    ]
    live_slots = jnp.arange(slot_total)[None, :] < counts[:, row_index, column_index][:, None]
    grid_cols = BLOCK * column_devices
    grid_row = group_cells // grid_cols
    grid_col = group_cells % grid_cols
    owner_tile = grid_row // BLOCK // row_devices
    local_cell = grid_row % BLOCK * BLOCK + grid_col % BLOCK
    mine_mask = live_slots & (owner_tile == tile_index)
    cell_ids = jnp.arange(BLOCK * BLOCK)
    my_owner = owner_tile[tile_index]
    my_live = live_slots[tile_index]
    selector = ((my_owner[None, :] == jnp.arange(tile_devices)[:, None]) & my_live[None, :]).astype(
        jnp.bfloat16
    )
    outgoing = jnp.dot(selector, encoded, preferred_element_type=jnp.float32).astype(jnp.bfloat16)
    incoming = lax.all_to_all(outgoing, "tile", split_axis=0, concat_axis=0, tiled=True)
    placement = jnp.any(
        (local_cell[None, :, :] == cell_ids[:, None, None]) & mine_mask[None, :, :], axis=2
    ).astype(jnp.bfloat16)
    block_cells = jnp.dot(placement, incoming, preferred_element_type=jnp.float32)
    grid_tokens = block_cells.astype(jnp.bfloat16).reshape(BLOCK, BLOCK, width_model)
    slide_in = layer_norm(block_cells, slide_gain, 1e-05).astype(jnp.bfloat16)
    slide_query = jnp.dot(slide_in, slide_full[0], preferred_element_type=jnp.float32).astype(
        jnp.bfloat16
    )
    slide_keys = jnp.dot(slide_in, slide_full[1], preferred_element_type=jnp.float32).astype(
        jnp.bfloat16
    )
    slide_values = jnp.dot(slide_in, slide_full[2], preferred_element_type=jnp.float32).astype(
        jnp.bfloat16
    )
    inner_width = slide_keys.shape[1]
    key_value_cells = jnp.concatenate([slide_keys, slide_values], axis=1).reshape(
        BLOCK, BLOCK, 2 * inner_width
    )
    surround = with_halo(key_value_cells, ((("tile", "row"), 0), ("col", 1)), BLOCK)
    near_rows = surround.reshape(-1, 2 * inner_width)
    near_keys = near_rows[:, :inner_width]
    near_values = near_rows[:, inner_width:]
    block_row = tile_index * row_devices + row_index
    padded = jnp.pad(occupancy, BLOCK)
    window = lax.dynamic_slice(
        padded, (block_row * BLOCK, column_index * BLOCK), (3 * BLOCK, 3 * BLOCK)
    )
    mask_row = block_mask.reshape(-1)
    mask_grid = jnp.concatenate([mask_row[:4], jnp.ones((1,), jnp.int32), mask_row[4:]]).reshape(
        3, 3
    )
    mask_cells = jnp.repeat(jnp.repeat(mask_grid, BLOCK, axis=0), BLOCK, axis=1)
    usable = (window * mask_cells).reshape(-1) > 0
    query_live = (
        lax.dynamic_slice(occupancy, (block_row * BLOCK, column_index * BLOCK), (BLOCK, BLOCK))
        .reshape(-1)
        .astype(jnp.float32)
    )
    head_count = inner_width // HDS
    scores = jnp.einsum(
        "qhd,khd->hqk",
        slide_query.reshape(-1, head_count, HDS),
        near_keys.reshape(-1, head_count, HDS),
        preferred_element_type=jnp.float32,
    ) / math.sqrt(HDS)
    allow = usable[None, None, :]
    row_peak = jnp.max(jnp.where(allow, scores, -1e30), axis=-1, keepdims=True)
    weights_exp = jnp.where(allow, jnp.exp(scores - row_peak), 0.0)
    live_query = query_live[None, :, None]
    soft = (
        weights_exp / (jnp.sum(weights_exp, axis=-1, keepdims=True) + 1.0 - live_query) * live_query
    ).astype(jnp.bfloat16)
    slide_mix = (
        jnp.einsum(
            "hqk,khd->qhd",
            soft,
            near_values.reshape(-1, head_count, HDS),
            preferred_element_type=jnp.float32,
        )
        .reshape(-1, inner_width)
        .astype(jnp.bfloat16)
    )
    slide_branch = contract_last(slide_mix, slide_full[3]).reshape(BLOCK, BLOCK, width_model)
    return (grid_tokens, slide_branch)


def solution(mesh):
    placed = (
        P(("tile", "row", "col"), None, None),
        P(),
        P(),
        P(),
        P(("tile", "row"), "col", None),
        P(),
        P("tile", None),
        P("tile", None),
        P("tile", None),
        P("tile", None),
        P(),
        P("tile", None),
        P(),
        P("tile", None),
        P("tile", None),
        P("tile", None),
        P("tile", None),
    )
    return jax.shard_map(
        local,
        mesh=mesh,
        in_specs=placed,
        out_specs=(P(("tile", "row"), "col", None), P(("tile", "row"), "col", None)),
        check_vma=False,
    )
```

profile of v0, /device:TPU:1, one launch (start us, length us, event | category | flops | bytes accessed | tf_op | source)
XLA Modules:
  0.0 334.1 jit_solution(3258398511303378004)
XLA Ops:
  7.3 0.7 all-gather.6.cloned.1.call-update
  8.0 0.7 all-gather.10.cloned.1.call-update
  8.8 0.7 all-gather.12.cloned.1.call-update
  9.5 0.5 all-gather.8.cloned.1.call-update
  10.1 0.5 all-gather.14.cloned.1.call-update
  10.6 0.7 reshape.291
  11.4 0.3 dynamic-slice_reduce_fusion.1
  11.7 0.6 dynamic_slice.33
  12.3 0.9 slice.22
  13.3 0.2 fusion.30
  13.5 0.8 reshape.290
  14.4 0.2 dynamic-slice_reduce_fusion.2
  14.6 0.2 dynamic-slice_reduce_fusion.3
  14.8 0.7 iota_compare_fusion.3
  15.5 30.2 %all_gather.33 = bf16[768,384]{1,0:T(8,128)(2,1)} all-gather(bf16[96,384]{1,0:T(8,128)(2,1)} %param.34), channel_id=1, replica_groups=mesh['tile'=8,'row'=2,'col'=2] {'tile'}, dimensions={0}, use_global_device_ids=true | all-gather | bytes 663552 | tf_op jit(solution)/shard_map/all_gather | solution.py:147
  45.7 29.5 %all_gather.32 = bf16[768,384]{1,0:T(8,128)(2,1)} all-gather(bf16[96,384]{1,0:T(8,128)(2,1)S(1)} %copy-done.5), channel_id=1, replica_groups=mesh['tile'=8,'row'=2,'col'=2] {'tile'}, dimensions={0}, use_global_device_ids=true | all-gather | bytes 663552 | tf_op jit(solution)/shard_map/all_gather | solution.py:146
  75.2 27.9 %all_gather.34 = bf16[768,384]{1,0:T(8,128)(2,1)} all-gather(bf16[96,384]{1,0:T(8,128)(2,1)S(1)} %copy-done.6), channel_id=1, replica_groups=mesh['tile'=8,'row'=2,'col'=2] {'tile'}, dimensions={0}, use_global_device_ids=true | all-gather | bytes 663552 | tf_op jit(solution)/shard_map/all_gather | solution.py:145
  103.4 29.4 %all_gather.35 = bf16[768,384]{1,0:T(8,128)(2,1)} all-gather(bf16[96,384]{1,0:T(8,128)(2,1)S(1)} %copy-done.7), channel_id=1, replica_groups=mesh['tile'=8,'row'=2,'col'=2] {'tile'}, dimensions={0}, use_global_device_ids=true | all-gather | bytes 663552 | tf_op jit(solution)/shard_map/all_gather | solution.py:148
  132.8 2.1 convolution_convert_fusion.5
  135.0 0.2 all-gather.10.cloned.1.call-done
  135.2 53.2 %all-gather.12.cloned.1.call-done = bf16[1536,768]{1,0:T(8,128)(2,1)} async-done(((bf16[192,768]{1,0:T(8,128)(2,1)}), bf16[1536,768]{1,0:T(8,128)(2,1)}) %all-gather.12.cloned.1.call-update) | async-done | bytes 2359312 | tf_op jit(solution)/shard_map/all_gather | solution.py:135
  188.3 52.7 %all-gather.8.cloned.1.call-done = bf16[1536,768]{1,0:T(8,128)(2,1)} async-done(((bf16[192,768]{1,0:T(8,128)(2,1)}), bf16[1536,768]{1,0:T(8,128)(2,1)}) %all-gather.8.cloned.1.call-update) | async-done | bytes 2359312 | tf_op jit(solution)/shard_map/all_gather | solution.py:129
  241.0 34.7 %while.10 = (s32[]{:T(128)}, f32[3,1536]{1,0:T(4,128)S(1)}, s32[]{:T(128)}, bf16[3,768]{1,0:T(4,128)(2,1)S(1)}, bf16[3,256,1536]{2,1,0:T(8,128)(2,1)}, /*index=5...) while((s32[]{:T(128)}, f32[3,1536]{1,0:T(4,128)S(1)}, ...), condition=%wide.region_8.9_spmd, body=%wide.region_3.8_spmd.sunk | while | flops 1217817856 | bytes 22927292 | solution.py:87
  241.7 1.3 convert_reduce_fusion.3
  243.0 1.5 fusion.126
  244.5 2.8 convolution_convert_fusion.12
  247.9 0.2 fusion.129
  248.2 2.9 convolution_convert_fusion.11
  251.3 0.2 fusion.131
  251.6 0.7 fusion.132
  253.1 1.3 convert_reduce_fusion.3
  254.4 1.5 fusion.126
  255.9 2.8 convolution_convert_fusion.12
  259.2 0.2 fusion.129
  259.5 2.9 convolution_convert_fusion.11
  262.6 0.2 fusion.131
  262.9 0.7 fusion.132
  264.4 1.3 convert_reduce_fusion.3
  265.7 1.5 fusion.126
  267.2 2.8 convolution_convert_fusion.12
  270.6 0.2 fusion.129
  270.9 2.9 convolution_convert_fusion.11
  274.0 0.2 fusion.131
  274.3 0.7 fusion.132
  275.9 0.2 multiply_reduce_fusion
  276.1 17.8 %all-gather.14.cloned.1.call-done = bf16[1536,768]{1,0:T(8,128)(2,1)} async-done(((bf16[192,768]{1,0:T(8,128)(2,1)}), bf16[1536,768]{1,0:T(8,128)(2,1)}) %all-gather.14.cloned.1.call-update) | async-done | bytes 2359312 | tf_op jit(solution)/shard_map/all_gather | solution.py:136
  293.9 2.2 fusion.19
  296.2 0.5 broadcast.385
  296.7 0.6 reduce.10
  297.4 0.6 reshape.316
  298.0 4.1 %all-to-all-start = ((bf16[8,2,384]{2,1,0:T(2,128)(2,1)}), bf16[8,2,384]{2,1,0:T(2,128)(2,1)S(1)}, u32[]{:S(2)}, u32[]{:S(2)}) async-start(bf16[8,2,384]{2,1,0:T(2,128)(2,1)} %reshape.316), calls=%async_computation | async-start | bytes 24576 | tf_op jit(solution)/shard_map/all_to_all | solution.py:172
  302.1 5.4 %all-to-all-done = bf16[8,2,384]{2,1,0:T(2,128)(2,1)S(1)} async-done(((bf16[8,2,384]{2,1,0:T(2,128)(2,1)}), bf16[8,2,384]{2,1,0:T(2,128)(2,1)S(1)}, u32[]{:S(2)}, u32[]{:S(2)}) %all-to-all-start) | async-done | bytes 12320 | tf_op jit(solution)/shard_map/all_to_all | solution.py:172
  307.5 0.2 fusion.78
  307.7 0.2 multiply_reduce_fusion.1
  308.5 4.2 %collective-permute-start = (bf16[2,2,768]{2,1,0:T(2,128)(2,1)S(1)}, bf16[2,2,768]{2,1,0:T(2,128)(2,1)S(1)}, u32[]{:S(2)}, u32[]{:S(2)}) collective-permute-start(bf16[2,2,768]{2,1,0:T(2,128)(2,1)S(1)} %reshape.293), channel_id=1, source_target_pairs={{0,2},{2,4},{4,6},{6,8},{8,10},{10,12},{12,14},{14,16},{16,18},{18... | collective-permute-start | bytes 18440 | tf_op jit(solution)/shard_map/ppermute | solution.py:21
  313.1 1.9 collective-permute-start.1
  315.1 3.0 collective-permute-done.1
  318.0 3.1 collective-permute-start.2
  321.1 1.3 collective-permute-start.3
  322.7 0.6 reshape.292
  323.3 2.3 collective-permute-done.3
  326.1 0.2 fusion.79
  326.3 0.3 fusion.20
  326.7 0.9 fusion.22
  (122 shorter events, 6.0 us)
Async XLA Ops:
  7.2 38.5 %copy-start.5 = (bf16[96,384]{1,0:T(8,128)(2,1)S(1)}, bf16[96,384]{1,0:T(8,128)(2,1)}, u32[]{:S(2)}) copy-start(bf16[96,384]{1,0:T(8,128)(2,1)} %param.33) | copy-start | bytes 221188
  7.2 68.0 %copy-start.6 = (bf16[96,384]{1,0:T(8,128)(2,1)S(1)}, bf16[96,384]{1,0:T(8,128)(2,1)}, u32[]{:S(2)}) copy-start(bf16[96,384]{1,0:T(8,128)(2,1)} %param.32) | copy-start | bytes 221188
  7.2 95.8 %copy-start.12 = (s32[1,1,8]{2,1,0:T(1,128)S(1)}, s32[1,1,8]{2,1,0:T(1,128)}, u32[]{:S(2)}) copy-start(s32[1,1,8]{2,1,0:T(1,128)} %param.23) | copy-start | bytes 100
  7.2 96.2 %copy-start.7 = (bf16[96,384]{1,0:T(8,128)(2,1)S(1)}, bf16[96,384]{1,0:T(8,128)(2,1)}, u32[]{:S(2)}) copy-start(bf16[96,384]{1,0:T(8,128)(2,1)} %param.35) | copy-start | bytes 221188
  7.2 125.5 %copy-start.10 = (s32[32,4]{0,1:T(4,128)S(1)}, s32[32,4]{0,1:T(4,128)}, u32[]{:S(2)}) copy-start(s32[32,4]{0,1:T(4,128)} %param.22) | copy-start | bytes 1540
  7.2 125.6 %copy-start.8 = (f32[1536]{0:T(1024)S(1)}, f32[1536]{0:T(1024)}, u32[]{:S(2)}) copy-start(f32[1536]{0:T(1024)} %param.24) | copy-start | bytes 18436
  7.2 125.6 %all-gather.6.cloned.1.call-start = ((), (), s32[]{:S(2)}) async-start(), calls=%async_computation.1 | async-start | bytes 2654208 | tf_op jit(solution)/shard_map/all_gather | solution.py:134
  8.0 127.2 %all-gather.10.cloned.1.call-start = ((), (), s32[]{:S(2)}) async-start(), calls=%async_computation.3 | async-start | bytes 2654208 | tf_op jit(solution)/shard_map/all_gather | solution.py:130
  8.7 179.6 %all-gather.12.cloned.1.call-start = ((), (), s32[]{:S(2)}) async-start(), calls=%async_computation.4 | async-start | bytes 2654208 | tf_op jit(solution)/shard_map/all_gather | solution.py:135
  9.4 231.6 %all-gather.8.cloned.1.call-start = ((), (), s32[]{:S(2)}) async-start(), calls=%async_computation.2 | async-start | bytes 2654208 | tf_op jit(solution)/shard_map/all_gather | solution.py:129
  10.0 283.9 %all-gather.14.cloned.1.call-start = ((), (), s32[]{:S(2)}) async-start(), calls=%async_computation.5 | async-start | bytes 2654208 | tf_op jit(solution)/shard_map/all_gather | solution.py:136
  241.0 52.9 %copy-start.9 = (f32[1536]{0:T(1024)S(1)}, f32[1536]{0:T(1024)}, u32[]{:S(2)}) copy-start(f32[1536]{0:T(1024)} %param.29) | copy-start | bytes 18436
  248.2 3.4 %copy-start = (bf16[1536,768]{1,0:T(8,128)(2,1)S(1)}, bf16[1536,768]{1,0:T(8,128)(2,1)}, u32[]{:S(2)}) copy-start(bf16[1536,768]{1,0:T(8,128)(2,1)} %get-tuple-element.170) | copy-start | bytes 7077892 | tf_op jit(solution)/shard_map/while
  259.5 3.4 %copy-start = (bf16[1536,768]{1,0:T(8,128)(2,1)S(1)}, bf16[1536,768]{1,0:T(8,128)(2,1)}, u32[]{:S(2)}) copy-start(bf16[1536,768]{1,0:T(8,128)(2,1)} %get-tuple-element.170) | copy-start | bytes 7077892 | tf_op jit(solution)/shard_map/while
  270.9 3.4 %copy-start = (bf16[1536,768]{1,0:T(8,128)(2,1)S(1)}, bf16[1536,768]{1,0:T(8,128)(2,1)}, u32[]{:S(2)}) copy-start(bf16[1536,768]{1,0:T(8,128)(2,1)} %get-tuple-element.170) | copy-start | bytes 7077892 | tf_op jit(solution)/shard_map/while
  275.7 32.2 %copy-start.11 = (f32[768]{0:T(1024)S(1)}, f32[768]{0:T(1024)}, u32[]{:S(2)}) copy-start(f32[768]{0:T(1024)} %param.31) | copy-start | bytes 9220
  275.8 32.3 %copy-start.4 = (bf16[768,384]{1,0:T(8,128)(2,1)S(1)}, bf16[768,384]{1,0:T(8,128)(2,1)}, u32[]{:S(2)}) copy-start(bf16[768,384]{1,0:T(8,128)(2,1)} %all_gather.33) | copy-start | bytes 1769476
  275.8 32.5 %copy-start.3 = (bf16[768,384]{1,0:T(8,128)(2,1)S(1)}, bf16[768,384]{1,0:T(8,128)(2,1)}, u32[]{:S(2)}) copy-start(bf16[768,384]{1,0:T(8,128)(2,1)} %all_gather.32) | copy-start | bytes 1769476
  275.8 46.6 %copy-start.2 = (bf16[768,384]{1,0:T(8,128)(2,1)S(1)}, bf16[768,384]{1,0:T(8,128)(2,1)}, u32[]{:S(2)}) copy-start(bf16[768,384]{1,0:T(8,128)(2,1)} %all_gather.34) | copy-start | bytes 1769476
  276.1 50.6 %copy-start.1 = (bf16[768,384]{1,0:T(8,128)(2,1)S(1)}, bf16[768,384]{1,0:T(8,128)(2,1)}, u32[]{:S(2)}) copy-start(bf16[768,384]{1,0:T(8,128)(2,1)} %all_gather.35) | copy-start | bytes 1769476
  298.0 9.5 %all-to-all-start = ((bf16[8,2,384]{2,1,0:T(2,128)(2,1)}), bf16[8,2,384]{2,1,0:T(2,128)(2,1)S(1)}, u32[]{:S(2)}, u32[]{:S(2)}) async-start(bf16[8,2,384]{2,1,0:T(2,128)(2,1)} %reshape.316), calls=%async_computation | async-start | bytes 24576 | tf_op jit(solution)/shard_map/all_to_all | solution.py:172
  308.5 6.5 %collective-permute-start = (bf16[2,2,768]{2,1,0:T(2,128)(2,1)S(1)}, bf16[2,2,768]{2,1,0:T(2,128)(2,1)S(1)}, u32[]{:S(2)}, u32[]{:S(2)}) collective-permute-start(bf16[2,2,768]{2,1,0:T(2,128)(2,1)S(1)} %reshape.293), channel_id=1, source_target_pairs={{0,2},{2,4},{4,6},{6,8},{8,10},{10,12},{12,14},{14,16},{16,18},{18... | collective-permute-start | bytes 18440 | tf_op jit(solution)/shard_map/ppermute | solution.py:21
  313.1 4.9 %collective-permute-start.1 = (bf16[2,2,768]{2,1,0:T(2,128)(2,1)S(1)}, bf16[2,2,768]{2,1,0:T(2,128)(2,1)S(1)}, u32[]{:S(2)}, u32[]{:S(2)}) collective-permute-start(bf16[2,2,768]{2,1,0:T(2,128)(2,1)S(1)} %reshape.293), channel_id=1, source_target_pairs={{2,0},{4,2},{6,4},{8,6},{10,8},{12,10},{14,12},{16,14},{18,16},{20... | collective-permute-start | bytes 18440 | tf_op jit(solution)/shard_map/ppermute | solution.py:23
  318.0 5.3 %collective-permute-start.2 = (bf16[6,2,768]{2,1,0:T(2,128)(2,1)S(1)}, bf16[6,2,768]{2,1,0:T(2,128)(2,1)S(1)}, u32[]{:S(2)}, u32[]{:S(2)}) collective-permute-start(bf16[6,2,768]{2,1,0:T(2,128)(2,1)S(1)} %constant_dynamic-update-slice_fusion), channel_id=1, source_target_pairs={{0,1},{2,3},{4,5},{6,7},{8,9},{10,11},{12,13},{14,15},{16,17},{18,... | collective-permute-start | bytes 55304 | tf_op jit(solution)/shard_map/ppermute | solution.py:21
  321.1 4.5 %collective-permute-start.3 = (bf16[6,2,768]{2,1,0:T(2,128)(2,1)S(1)}, bf16[6,2,768]{2,1,0:T(2,128)(2,1)S(1)}, u32[]{:S(2)}, u32[]{:S(2)}) collective-permute-start(bf16[6,2,768]{2,1,0:T(2,128)(2,1)S(1)} %constant_dynamic-update-slice_fusion), channel_id=1, source_target_pairs={{1,0},{3,2},{5,4},{7,6},{9,8},{11,10},{13,12},{15,14},{17,16},{19,... | collective-permute-start | bytes 55304 | tf_op jit(solution)/shard_map/ppermute | solution.py:23
Sparse Core Ops, SparseCore 0:
  10.2 62.8 all-gather.5
  75.3 59.7 all-gather.9
  137.4 50.9 all-gather.11
  190.4 50.6 all-gather.7
  243.1 50.8 all-gather.13
where the time goes:
time: 335 us; the launch traced here: 334 us
  waiting for transfers between devices  138 us (41%)
  blocking collectives  117 us (35%)
  matrix products  26.7 us (8%)
  starting transfers between devices  14.7 us (4%)
  between operations  14.1 us (4%)
  other arithmetic  12.5 us (4%)
  local copies, waits for them, and re-layouts  8.74 us (3%)
    all_gather x1, waiting for transfers between devices, local(): lax.all_gather(w_out_t, 'tile', axis=0, tiled=True)  53.2 us
    all_gather x1, waiting for transfers between devices, local(): lax.all_gather(w_key, 'tile', axis=0, tiled=True)  52.7 us
    all_gather x1, blocking collectives, local(): lax.all_gather(s_value, 'tile', axis=0, tiled=True)  30.2 us
    all_gather x1, blocking collectives, local(): lax.all_gather(s_key, 'tile', axis=0, tiled=True)  29.5 us
    all_gather x1, blocking collectives, local(): lax.all_gather(s_out_t, 'tile', axis=0, tiled=True)  29.4 us
    all_gather x1, blocking collectives, local(): lax.all_gather(s_query, 'tile', axis=0, tiled=True)  27.9 us
    all_gather x1, waiting for transfers between devices, local(): lax.all_gather(w_proj, 'tile', axis=0, tiled=True)  17.8 us
    dot_general x3, matrix products, class_branch(): jnp.dot(normed, value_part, preferred_element_type=jnp.float32)  8.72 us
  transfers between devices with their start and end apart: 10, of which 7 were waited for; matrix products, arithmetic and copies ran while one was open for 12% of the time, Pallas kernels for 0%

commit v1 on v0

--- a/solution.py
+++ b/solution.py
@@ -3,6 +3,8 @@
 import jax
 import jax.numpy as jnp
 from jax import lax
+from jax.experimental import pallas as pl
+from jax.experimental.pallas import tpu as pltpu
 from jax.sharding import PartitionSpec as P
 
 HD = 64
@@ -237,6 +239,564 @@
     return (grid_tokens, slide_branch)
 
 
+MESH_ID = pl.DeviceIdType.MESH
+NEAR = [(-1, -1), (-1, 0), (-1, 1), (0, -1), (0, 1), (1, -1), (1, 0), (1, 1)]
+FAR_BIAS = -1e30
+PHASES = 8
+
+
+def fits_fused(mesh):
+    return mesh.shape["tile"] == 8 and mesh.shape["row"] == 2
+
+
+def contract_rows(first_op, second_op):
+    return lax.dot_general(
+        first_op, second_op, (((1,), (1,)), ((), ())), preferred_element_type=jnp.float32
+    )
+
+
+def matmul(first_op, second_op):
+    return jnp.dot(first_op, second_op, preferred_element_type=jnp.float32)
+
+
+def fused_kernel(
+    sizes,
+    cell_ref,
+    count_ref,
+    mask_ref,
+    tok_hbm,
+    enc_gain_ref,
+    final_gain_ref,
+    slide_gain_ref,
+    wq_ref,
+    wk_ref,
+    wv_ref,
+    wo_ref,
+    wp_ref,
+    sq_ref,
+    sk_ref,
+    sv_ref,
+    so_ref,
+    grid_ref,
+    branch_ref,
+    cls,
+    tok,
+    normed,
+    s1,
+    r1,
+    s2,
+    r2,
+    s3,
+    r3,
+    s4,
+    r4,
+    s5,
+    r5,
+    s6,
+    r6,
+    s7,
+    r7,
+    s9,
+    r9,
+    sg,
+    rg,
+    halo_out,
+    halo,
+    wide,
+    gains,
+    live,
+    slide_w,
+    in_sem,
+    send_sem,
+    recv_sem,
+    w_send,
+    w_recv,
+    halo_send,
+    halo_recv,
+):
+    tiles, rows_n, cols_n, slots, patch, width, inner = sizes
+    shard = width // tiles
+    half = inner // 2
+    heads = inner // HD
+    half_heads = heads // 2
+    bf, f32 = jnp.bfloat16, jnp.float32
+    me = lax.axis_index("tile")
+    my_row = lax.axis_index("row")
+    my_col = lax.axis_index("col")
+    block_row = me * rows_n + my_row
+
+    first_in = pltpu.make_async_copy(tok_hbm.at[:, pl.ds(0, 16), :], cls, in_sem.at[0])
+    first_in.start()
+    whole_in = pltpu.make_async_copy(tok_hbm, tok, in_sem.at[1])
+    whole_in.start()
+
+    blank = jnp.where(
+        lax.broadcasted_iota(jnp.int32, (8, halo.shape[2]), 1) == halo_lane(halo), FAR_BIAS, 0.0
+    )
+    for place in range(9):
+        halo[place] = blank
+
+    barrier = pltpu.get_barrier_semaphore()
+    for step in range(1, tiles):
+        pl.semaphore_signal(
+            barrier, inc=1, device_id={"tile": lax.rem(me + step, tiles)}, device_id_type=MESH_ID
+        )
+    beside = []
+    near_count = jnp.int32(0)
+    for down, right in NEAR:
+        to_row = block_row + down
+        to_col = my_col + right
+        inside = (to_row >= 0) & (to_row < tiles * rows_n) & (to_col >= 0) & (to_col < cols_n)
+        target = {
+            "tile": lax.div(to_row + rows_n, rows_n) - 1,
+            "row": lax.rem(to_row + rows_n, rows_n),
+            "col": to_col,
+        }
+        beside.append((inside, target))
+        near_count = near_count + inside.astype(jnp.int32)
+
+        @pl.when(inside)
+        def greet(target=target):
+            pl.semaphore_signal(barrier, inc=1, device_id=target, device_id_type=MESH_ID)
+
+    first_in.wait()
+    raw = [cls[slot].astype(f32)[0:1] for slot in range(slots)]
+    raw_rows = jnp.concatenate(raw, axis=0)
+    enc_gain = enc_gain_ref[...]
+    class_normed = layer_norm(raw_rows, enc_gain, 1e-06).astype(bf).astype(f32)
+    class_rows = jnp.concatenate(
+        [class_normed, raw_rows, jnp.zeros((8 - 2 * slots, width), f32)], axis=0
+    )
+    for to in range(tiles):
+        s1[to, :, :shard] = class_rows[:, to * shard : (to + 1) * shard]
+        gains[to, :, :shard] = jnp.broadcast_to(
+            final_gain_ref[:, to * shard : (to + 1) * shard], (8, shard)
+        )
+
+    pl.semaphore_wait(barrier, tiles - 1 + near_count)
+
+    started = []
+
+    def send(phase, source, landing):
+        copies = []
+        for step in range(1, tiles):
+            to = lax.rem(me + step, tiles)
+            copy = pltpu.make_async_remote_copy(
+                src_ref=source.at[to] if len(source.shape) == len(landing.shape) else source,
+                dst_ref=landing.at[me],
+                send_sem=send_sem.at[phase, step],
+                recv_sem=recv_sem.at[phase, step],
+                device_id={"tile": to},
+                device_id_type=MESH_ID,
+            )
+            copy.start()
+            copies.append(copy)
+        started.extend(copies)
+        landing[me] = source[me] if len(source.shape) == len(landing.shape) else source[...]
+        return copies
+
+    def arrive(copies):
+        for copy in copies:
+            copy.wait_recv()
+
+    copies1 = send(0, s1, r1)
+
+    own_pair = pl.ds(my_row * 2, 2)
+    first_core = my_row == 0
+    slide_w[my_row * 2, me] = jnp.where(first_core, sq_ref[...], sv_ref[...])
+    slide_w[my_row * 2 + 1, me] = jnp.where(first_core, sk_ref[...], so_ref[...])
+    w_copies = []
+    for step in range(1, tiles):
+        copy = pltpu.make_async_remote_copy(
+            src_ref=slide_w.at[own_pair, me],
+            dst_ref=slide_w.at[own_pair, me],
+            send_sem=w_send.at[step],
+            recv_sem=w_recv.at[step],
+            device_id={"tile": lax.rem(me + step, tiles)},
+            device_id_type=MESH_ID,
+        )
+        copy.start()
+        w_copies.append(copy)
+
+    row64 = lax.broadcasted_iota(jnp.int32, (8 * tiles, 1), 0)
+    in_block = lax.rem(row64, 8)
+
+    def norm_chunk(chunk, carry):
+        rows = pl.ds(pl.multiple_of(chunk * 32, 32), 32)
+        inside = pl.ds(pl.multiple_of(lax.rem(chunk, per_tile) * 32, 32), 32)
+        wide_rows_in = tok[lax.div(chunk, per_tile), inside, :].astype(f32)
+        normed[rows, :] = layer_norm(wide_rows_in, enc_gain, 1e-06).astype(bf)
+        return carry
+
+    per_tile = patch // 32
+    whole_chunks = slots * per_tile
+    whole_in.wait()
+    my_gain = gains[me][:, :shard]
+    gain_high = my_gain.astype(bf)
+    gain_low = (my_gain - gain_high.astype(f32)).astype(bf)
+    sums = [
+        matmul(gain_high, wp_ref[:, cut : cut + half])
+        + matmul(gain_low, wp_ref[:, cut : cut + half])
+        for cut in (0, half)
+    ]
+    low_rows = lax.broadcasted_iota(jnp.int32, (8, 1), 0) < 4
+    sg[...] = jnp.where(low_rows, sums[0], sums[1])
+    copies_g = send(7, sg, rg)
+
+    col64 = lax.broadcasted_iota(jnp.int32, (8 * tiles, 8 * tiles), 1)
+    row_full = lax.broadcasted_iota(jnp.int32, (8 * tiles, 8 * tiles), 0)
+    place_low = jnp.zeros((8 * tiles, 8 * tiles), f32)
+    grid_cols = BLOCK * cols_n
+    group = my_row * cols_n + my_col
+    row_key = lax.div(row_full, 8) * 4 + lax.rem(row_full, 4)
+    for other in range(tiles):
+        device = other * rows_n * cols_n + group
+        count = count_ref[device]
+        for slot in range(slots):
+            cell = cell_ref[device * slots + slot]
+            cell_row = lax.div(cell, jnp.int32(grid_cols))
+            cell_col = lax.rem(cell, jnp.int32(grid_cols))
+            owner = lax.div(cell_row, jnp.int32(BLOCK * rows_n))
+            spot = owner * 4 + lax.rem(cell_row, BLOCK) * BLOCK + lax.rem(cell_col, BLOCK)
+            spot = jnp.where(slot < count, spot, -1)
+            hit = (row_key == spot) & (col64 == other * 8 + slot)
+            place_low = jnp.where(hit, 1.0, place_low)
+    place_high = jnp.concatenate([jnp.zeros((8 * tiles, slots), f32), place_low[:, :-slots]], axis=1)
+    live_col = jnp.sum(place_low, axis=1, keepdims=True)
+    live[...] = jnp.broadcast_to(live_col, (8 * tiles, 128)).reshape(tiles, 8, 128)
+    place_low = place_low.astype(bf)
+    place_high = place_high.astype(bf)
+
+    arrive(copies1)
+    shards1 = r1[...].reshape(8 * tiles, r1.shape[2])[:, :shard].astype(bf)
+    part_low = matmul(shards1, wq_ref[:, :half])
+    part_high = matmul(shards1, wq_ref[:, half:])
+    shifted = jnp.concatenate([part_high[-slots:], part_high[:-slots]], axis=0)
+    s2[...] = jnp.where(in_block < slots, part_low, shifted).reshape(s2.shape)
+    copies2 = send(1, s2, r2)
+    lax.fori_loop(0, whole_chunks // 3, norm_chunk, 0)
+    arrive(copies2)
+    s3[...] = jnp.sum(r2[...], axis=0).astype(bf).astype(f32)
+    copies3 = send(2, s3, r3)
+    lax.fori_loop(whole_chunks // 3, 2 * (whole_chunks // 3), norm_chunk, 0)
+
+    wide_rows = 48 * tiles
+    exp_row = lax.broadcasted_iota(jnp.int32, (wide_rows, 8 * tiles), 0)
+    exp_col = lax.broadcasted_iota(jnp.int32, (wide_rows, 8 * tiles), 1)
+    exp_in = lax.rem(exp_row, 48)
+    exp_slot = lax.div(exp_in, heads)
+    exp_head = lax.rem(exp_in, heads)
+    exp_base = lax.div(exp_row, 48) * 8 + exp_slot
+    real = exp_slot < slots
+    pick_low = (real & (exp_head < half_heads) & (exp_col == exp_base)).astype(f32).astype(bf)
+    pick_high = (
+        (real & (exp_head >= half_heads) & (exp_col == exp_base + slots)).astype(f32).astype(bf)
+    )
+    head_of_row = lax.rem(
+        lax.rem(lax.broadcasted_iota(jnp.int32, (wide_rows, half), 0), 48), heads
+    )
+    head_of_col = lax.div(lax.broadcasted_iota(jnp.int32, (wide_rows, half), 1), HD)
+    own_low = head_of_row == head_of_col
+    own_high = head_of_row == head_of_col + half_heads
+    arrive(copies3)
+    queries = r3[...].reshape(8 * tiles, half).astype(bf)
+    query_low = jnp.where(own_low, matmul(pick_low, queries), 0.0).astype(bf)
+    query_high = jnp.where(own_high, matmul(pick_high, queries), 0.0).astype(bf)
+    folded = contract_rows(query_low, wk_ref[:, :half]) + contract_rows(
+        query_high, wk_ref[:, half:]
+    )
+    s4[:, :, :shard] = folded.astype(bf).reshape(tiles, 48, shard)
+    copies4 = send(3, s4, r4)
+    lax.fori_loop(2 * (whole_chunks // 3), whole_chunks, norm_chunk, 0)
+    arrive(copies4)
+
+    for other in range(tiles):
+        wide[:, other * shard : (other + 1) * shard] = r4[other, :, :shard]
+    tokens = normed[...]
+    scores = contract_rows(wide[...], tokens) / math.sqrt(HD)
+    score_slot = lax.div(lax.broadcasted_iota(jnp.int32, scores.shape, 0), heads)
+    score_tile = lax.div(lax.broadcasted_iota(jnp.int32, scores.shape, 1), patch)
+    same = score_slot == score_tile
+    peak = jnp.max(jnp.where(same, scores, -1e30), axis=1, keepdims=True)
+    grown = jnp.where(same, jnp.exp(jnp.minimum(scores - peak, 0.0)), 0.0)
+    total = jnp.sum(grown, axis=1, keepdims=True)
+    probs = (grown / jnp.where(total > 0.0, total, 1.0)).astype(bf)
+    mixed = matmul(probs, tokens).astype(bf)
+    for to in range(tiles):
+        s5[to, :, :shard] = mixed[:, to * shard : (to + 1) * shard]
+    copies5 = send(4, s5, r5)
+    arrive(copies5)
+
+    mixes = r5[...].reshape(wide_rows, r5.shape[2])[:, :shard]
+    value_low = jnp.where(own_low, matmul(mixes, wv_ref[:, :half]), 0.0).astype(bf)
+    value_high = jnp.where(own_high, matmul(mixes, wv_ref[:, half:]), 0.0).astype(bf)
+    columns0 = (((0,), (0,)), ((), ()))
+    gathered = lax.dot_general(
+        pick_low, value_low, columns0, preferred_element_type=f32
+    ) + lax.dot_general(pick_high, value_high, columns0, preferred_element_type=f32)
+    s6[...] = gathered.reshape(s6.shape)
+    copies6 = send(5, s6, r6)
+    arrive(copies6)
+    s7[...] = jnp.sum(r6[...], axis=0).astype(bf).astype(f32)
+    copies7 = send(6, s7, r7)
+    raw_cells = matmul(place_high, shards1)
+
+    for copy in w_copies:
+        copy.wait_recv()
+    pair_copy = pltpu.make_async_remote_copy(
+        src_ref=slide_w.at[own_pair],
+        dst_ref=slide_w.at[own_pair],
+        send_sem=w_send.at[0],
+        recv_sem=w_recv.at[0],
+        device_id={"row": 1 - my_row},
+        device_id_type=MESH_ID,
+    )
+    pair_copy.start()
+    arrive(copies7)
+
+    mix_rows = r7[...].reshape(8 * tiles, half).astype(bf)
+    cell_low = matmul(place_low, mix_rows).astype(bf)
+    cell_high = matmul(place_high, mix_rows).astype(bf)
+    carried = (
+        raw_cells
+        + contract_rows(cell_low, wo_ref[:, :half])
+        + contract_rows(cell_high, wo_ref[:, half:])
+    )
+    part_mean = jnp.mean(carried, axis=1, keepdims=True)
+    centered = carried - part_mean
+    part_square = jnp.sum(centered * centered, axis=1, keepdims=True)
+    scaled = (centered * my_gain[0:1]).astype(bf)
+    landed = jnp.where(
+        in_block < 4, matmul(scaled, wp_ref[:, :half]), matmul(scaled, wp_ref[:, half:])
+    )
+    s9[:, :, :half] = landed.reshape(tiles, 8, half)
+    lane = lax.broadcasted_iota(jnp.int32, (8 * tiles, 128), 1)
+    s9[:, :, half:] = jnp.where(lane == 0, part_mean, part_square).reshape(tiles, 8, 128)
+    copies9 = send(8, s9, r9)
+    arrive(copies_g)
+    arrive(copies9)
+
+    means = [r9[other, :, half : half + 1] for other in range(tiles)]
+    mean = sum(means) / tiles
+    square = sum(
+        r9[other, :, half + 1 : half + 2] + shard * (means[other] - mean) ** 2
+        for other in range(tiles)
+    )
+    joined = sum(
+        r9[other, :, :half] + (means[other] - mean) * rg[other] for other in range(tiles)
+    )
+    joined = (joined * lax.rsqrt(square / width + 1e-06)).astype(bf)
+    cells32 = joined.astype(f32)
+    cells = jnp.concatenate([cells32[0:4], cells32[4:8]], axis=1)
+    grid_ref[0] = cells[0:2].astype(bf)
+    grid_ref[1] = cells[2:4].astype(bf)
+
+    pair_copy.wait_recv()
+    inner_s = so_ref.shape[1]
+    slide_rows = jnp.concatenate([cells, cells], axis=0)
+    slide_in = layer_norm(slide_rows, slide_gain_ref[...], 1e-05).astype(bf)
+
+    def slide_full(which):
+        return slide_w[which].reshape(-1, inner_s)
+
+    keys = matmul(slide_in, slide_full(1))
+    values = matmul(slide_in, slide_full(2))
+    my_live = live[me][:, 0:1]
+    halo_out[:, :inner_s] = jnp.where(low_rows, keys, values).astype(bf).astype(f32)
+    lane8 = lax.broadcasted_iota(jnp.int32, (8, 128), 1)
+    halo_out[:, inner_s:] = jnp.where(
+        (lane8 == 0) & jnp.logical_not(low_rows & (my_live > 0.0)), FAR_BIAS, 0.0
+    )
+    places = [0, 1, 2, 3, 5, 6, 7, 8]
+    halo_copies = []
+    for index, (inside, target) in enumerate(beside):
+        copy = pltpu.make_async_remote_copy(
+            src_ref=halo_out,
+            dst_ref=halo.at[8 - places[index]],
+            send_sem=halo_send.at[index],
+            recv_sem=halo_recv.at[7 - index],
+            device_id=target,
+            device_id_type=MESH_ID,
+        )
+
+        @pl.when(inside)
+        def send_halo(copy=copy):
+            copy.start()
+
+        halo_copies.append(copy)
+    halo[4] = halo_out[...]
+    slide_query = matmul(slide_in, slide_full(0)).astype(bf).astype(f32)
+    slide_heads = inner_s // HDS
+    head_lane = lax.div(lax.broadcasted_iota(jnp.int32, (8, inner_s), 1), HDS)
+    one_lane = jnp.where(lane8 == 0, math.sqrt(HDS), 0.0)
+    query_heads = jnp.concatenate(
+        [
+            jnp.concatenate([jnp.where(head_lane == head, slide_query, 0.0), one_lane], axis=1)
+            for head in range(slide_heads)
+        ],
+        axis=0,
+    ).astype(bf)
+    for index, (inside, target) in enumerate(beside):
+        arriving = pltpu.make_async_remote_copy(
+            src_ref=halo_out,
+            dst_ref=halo.at[places[index]],
+            send_sem=halo_send.at[index],
+            recv_sem=halo_recv.at[index],
+            device_id=target,
+            device_id_type=MESH_ID,
+        )
+
+        @pl.when(inside)
+        def take_halo(arriving=arriving):
+            arriving.wait_recv()
+
+    lane_wide = lax.broadcasted_iota(jnp.int32, (8, halo.shape[2]), 1)
+    near = []
+    for place in range(9):
+        rows = halo[place]
+        if place != 4:
+            shut = mask_ref[0, 0, places.index(place)] == 0
+            rows = jnp.where((lane_wide == inner_s) & shut, FAR_BIAS, rows)
+        near.append(rows)
+    near = jnp.concatenate(near, axis=0)
+    near_keys = near.astype(bf)
+    near_values = jnp.concatenate([near[4:], near[:4]], axis=0)[:, :inner_s].astype(bf)
+    slide_scores = contract_rows(query_heads, near_keys) / math.sqrt(HDS)
+    slide_peak = jnp.max(slide_scores, axis=1, keepdims=True)
+    slide_exp = jnp.exp(slide_scores - slide_peak)
+    alive = jnp.concatenate([my_live] * slide_heads, axis=0)
+    soft = (
+        slide_exp / (jnp.sum(slide_exp, axis=1, keepdims=True) + 1.0 - alive) * alive
+    ).astype(bf)
+    mix_heads = matmul(soft, near_values)
+    slide_mix = sum(
+        jnp.where(head_lane == head, mix_heads[8 * head : 8 * head + 8], 0.0)
+        for head in range(slide_heads)
+    ).astype(bf)
+    branch = contract_rows(slide_mix, slide_full(3))
+    branch_ref[0] = branch[0:2]
+    branch_ref[1] = branch[2:4]
+
+    for copy in started + w_copies + [pair_copy]:
+        copy.wait_send()
+    for (inside, target), copy in zip(beside, halo_copies):
+
+        @pl.when(inside)
+        def sent_halo(copy=copy):
+            copy.wait_send()
+
+
+def halo_lane(halo):
+    return halo.shape[2] - 128
+
+
+def fused(
+    tile_tokens,
+    tile_count,
+    tile_cell,
+    occupancy,
+    block_mask,
+    enc_gain,
+    w_query,
+    w_key,
+    w_value,
+    w_out_t,
+    final_gain,
+    w_proj,
+    slide_gain,
+    s_query,
+    s_key,
+    s_value,
+    s_out_t,
+):
+    tiles = lax.axis_size("tile")
+    rows_n = lax.axis_size("row")
+    cols_n = lax.axis_size("col")
+    slots, patch, width = tile_tokens.shape
+    inner = w_query.shape[1]
+    model = w_proj.shape[1]
+    inner_s = s_query.shape[1]
+    half = inner // 2
+    sizes = (tiles, rows_n, cols_n, slots, patch, width, inner)
+    bf, f32 = jnp.bfloat16, jnp.float32
+    vmem = pl.BlockSpec(memory_space=pltpu.VMEM)
+    smem = pl.BlockSpec(memory_space=pltpu.SMEM)
+    slab = pltpu.VMEM((tiles, 8, 256), f32)
+    packed = pltpu.VMEM((tiles, 8, half), f32)
+    one_packed = pltpu.VMEM((8, half), f32)
+    heads_slab = pltpu.VMEM((tiles, 48, 256), bf)
+    stat_slab = pltpu.VMEM((tiles, 8, half + 128), f32)
+
+    def kernel(*refs):
+        fused_kernel(sizes, *refs)
+
+    return pl.pallas_call(
+        kernel,
+        out_shape=(
+            jax.ShapeDtypeStruct((BLOCK, BLOCK, model), bf),
+            jax.ShapeDtypeStruct((BLOCK, BLOCK, model), f32),
+        ),
+        in_specs=[smem] * 3 + [pl.BlockSpec(memory_space=pl.ANY)] + [vmem] * 12,
+        out_specs=(vmem, vmem),
+        scratch_shapes=[
+            pltpu.VMEM((slots, 16, width), bf),
+            pltpu.VMEM((slots, patch, width), bf),
+            pltpu.VMEM((slots * patch, width), bf),
+            slab,
+            slab,
+            packed,
+            packed,
+            one_packed,
+            packed,
+            heads_slab,
+            heads_slab,
+            heads_slab,
+            heads_slab,
+            packed,
+            packed,
+            one_packed,
+            packed,
+            stat_slab,
+            stat_slab,
+            one_packed,
+            packed,
+            pltpu.VMEM((8, inner_s + 128), f32),
+            pltpu.VMEM((9, 8, inner_s + 128), f32),
+            pltpu.VMEM((48, width), bf),
+            slab,
+            pltpu.VMEM((tiles, 8, 128), f32),
+            pltpu.VMEM((4, tiles, s_query.shape[0], inner_s), bf),
+            pltpu.SemaphoreType.DMA((2,)),
+            pltpu.SemaphoreType.DMA((PHASES + 1, tiles)),
+            pltpu.SemaphoreType.DMA((PHASES + 1, tiles)),
+            pltpu.SemaphoreType.DMA((tiles,)),
+            pltpu.SemaphoreType.DMA((tiles,)),
+            pltpu.SemaphoreType.DMA((8,)),
+            pltpu.SemaphoreType.DMA((8,)),
+        ],
+        compiler_params=pltpu.CompilerParams(
+            collective_id=0, has_side_effects=True, vmem_limit_bytes=48 * 1024 * 1024
+        ),
+    )(
+        tile_cell,
+        tile_count,
+        block_mask,
+        tile_tokens,
+        enc_gain.reshape(1, width),
+        final_gain.reshape(1, width),
+        slide_gain.reshape(1, model),
+        w_query,
+        w_key,
+        w_value,
+        w_out_t,
+        w_proj,
+        s_query,
+        s_key,
+        s_value,
+        s_out_t,
+    )
+
+
 def solution(mesh):
     placed = (
         P(("tile", "row", "col"), None, None),
@@ -257,8 +817,9 @@
         P("tile", None),
         P("tile", None),
     )
+    per_device = fused if fits_fused(mesh) else local
     return jax.shard_map(
-        local,
+        per_device,
         mesh=mesh,
         in_specs=placed,
         out_specs=(P(("tile", "row"), "col", None), P(("tile", "row"), "col", None)),

time: 335 us -> 94.6 us (0.28)
  waiting for transfers between devices: 138 us -> 0 us
  blocking collectives: 117 us -> 0 us
  Pallas kernels: 0 us -> 78 us
  matrix products: 26.7 us -> 0 us
  starting transfers between devices: 14.7 us -> 0 us
  between operations: 14.1 us -> 0.65 us
  other arithmetic: 12.5 us -> 0 us
  local copies, waits for them, and re-layouts: 8.74 us -> 15.3 us
    all_gather x5 -> x0, waiting for transfers between devices: 124 us -> none  [the longest x1 53.2 us: local(): lax.all_gather(w_out_t, 'tile', axis=0, tiled=True)]
    all_gather x4 -> x0, blocking collectives: 117 us -> none  [the longest x1 30.2 us: local(): lax.all_gather(s_value, 'tile', axis=0, tiled=True)]
    pallas_call x0 -> x1, Pallas kernels: none -> 78 us  [fused(): pl.pallas_call(kernel, out_shape=(jax.ShapeDtypeStruct((BLOCK, BLOCK, mod...]
    dot_general x24 -> x0, matrix products: 26.7 us -> none  [the longest x3 8.72 us: class_branch(): jnp.dot(normed, value_part, preferred_element_type=jnp.float32)]
    unnamed x28, local copies, waits for them, and re-layouts: 0.72 us -> 13.2 us
    ppermute x4 -> x0, starting transfers between devices: 10.4 us -> none  [the longest x2 7.23 us: with_halo(): lax.ppermute(tail, axis, [(i, (i + 1) % count) for i in range(ends)])]
    reduce_sum x14 -> x0, other arithmetic: 9.82 us -> none  [the longest x6 5.04 us: layer_norm(): spread = jnp.mean(centered * centered, axis=-1, keepdims=True)]
    all_to_all x1 -> x0, waiting for transfers between devices: 5.38 us -> none  [local(): lax.all_to_all(outgoing, 'tile', split_axis=0, concat_axis=0, tiled=True)]
  transfers between devices with their start and end apart: 10 -> 0, of which waited for: 7 -> 0; matrix products, arithmetic and copies ran while one was open for 12% -> 0% of each run, Pallas kernels for 0% -> 0%
where the time goes in v1:
time: 94.6 us; the launch traced here: 93.9 us
  Pallas kernels  78 us (82%)
  local copies, waits for them, and re-layouts  15.3 us (16%)
    pallas_call x1, Pallas kernels, fused(): pl.pallas_call(kernel, out_shape=(jax.ShapeDtypeStruct((BLOCK, BLOCK, mod...  78 us
    unnamed x28, local copies, waits for them, and re-layouts  13.2 us

profile of v1, /device:TPU:1, one launch (start us, length us, event | category | flops | bytes accessed | tf_op | source)
XLA Modules:
  0.0 93.9 jit_solution(13999223661645763592)
XLA Ops:
  0.6 0.7 reshape.15.refs_6_
  1.3 0.7 reshape.13.refs_4_
  2.0 0.7 reshape.14.refs_5_
  2.7 0.0 copy-start
  2.7 1.7 %copy-done = bf16[3,256,1536]{2,1,0:T(8,128)(2,1)S(1)} copy-done((bf16[3,256,1536]{2,1,0:T(8,128)(2,1)S(1)}, bf16[3,256,1536]{2,1,0:T(8,128)(2,1)}, u32[]{:S(2)}) %copy-start) | copy-done | bytes 2359320
  4.4 0.0 copy-start.1
  4.4 1.0 %copy-done.1 = bf16[192,768]{1,0:T(8,128)(2,1)S(1)} copy-done((bf16[192,768]{1,0:T(8,128)(2,1)S(1)}, bf16[192,768]{1,0:T(8,128)(2,1)}, u32[]{:S(2)}) %copy-start.1) | copy-done | bytes 294936
  5.4 0.0 copy-start.2
  5.4 1.0 %copy-done.2 = bf16[192,768]{1,0:T(8,128)(2,1)S(1)} copy-done((bf16[192,768]{1,0:T(8,128)(2,1)S(1)}, bf16[192,768]{1,0:T(8,128)(2,1)}, u32[]{:S(2)}) %copy-start.2) | copy-done | bytes 294936
  6.3 0.0 copy-start.3
  6.3 1.0 %copy-done.3 = bf16[192,768]{1,0:T(8,128)(2,1)S(1)} copy-done((bf16[192,768]{1,0:T(8,128)(2,1)S(1)}, bf16[192,768]{1,0:T(8,128)(2,1)}, u32[]{:S(2)}) %copy-start.3) | copy-done | bytes 294936
  7.3 0.0 copy-start.4
  7.3 1.0 %copy-done.4 = bf16[192,768]{1,0:T(8,128)(2,1)S(1)} copy-done((bf16[192,768]{1,0:T(8,128)(2,1)S(1)}, bf16[192,768]{1,0:T(8,128)(2,1)}, u32[]{:S(2)}) %copy-start.4) | copy-done | bytes 294936
  8.2 0.0 copy-start.5
  8.2 1.0 %copy-done.5 = bf16[192,768]{1,0:T(8,128)(2,1)S(1)} copy-done((bf16[192,768]{1,0:T(8,128)(2,1)S(1)}, bf16[192,768]{1,0:T(8,128)(2,1)}, u32[]{:S(2)}) %copy-start.5) | copy-done | bytes 294936
  9.2 0.0 copy-start.6
  9.2 0.9 copy-done.6
  10.1 0.0 copy-start.7
  10.1 0.9 copy-done.7
  11.0 0.0 copy-start.8
  11.0 0.9 copy-done.8
  11.9 0.0 copy-start.9
  11.9 0.9 copy-done.9
  12.7 0.0 copy-start.10
  12.7 0.7 copy-done.10
  13.4 0.0 copy-start.11
  13.4 0.7 copy-done.11
  14.1 0.0 copy-start.12
  14.1 0.7 copy-done.12
  14.7 78.0 %shard_map.167 = (bf16[2,2,768]{2,1,0:T(2,128)(2,1)S(1)}, f32[2,2,768]{2,1,0:T(2,128)S(1)}) custom-call(s32[96]{0:T(128)S(1)} %copy-done.10, s32[32]{0:T(128)S(1)} %copy-done.11, s32[1,1,8]{2,1,0:T(1,128)S(1)} %copy-done.12, bf16[3,256,1536]{2,1,0:T(8,128)(2,1)S(1)} %copy-done, f32[1,1536]{1,0:T(1,128)S(1)} %reshape.13.refs_4_, ...), custom_call_target="tpu_custom_call" | custom-call | tf_op jit(solution)/shard_map/pallas_call | solution.py:733
  92.7 0.6 copy.20
  93.3 0.6 copy.21
Async XLA Ops:
  2.7 1.7 %copy-start = (bf16[3,256,1536]{2,1,0:T(8,128)(2,1)S(1)}, bf16[3,256,1536]{2,1,0:T(8,128)(2,1)}, u32[]{:S(2)}) copy-start(bf16[3,256,1536]{2,1,0:T(8,128)(2,1)} %refs_3_.1) | copy-start | bytes 7077892
  4.4 1.0 %copy-start.1 = (bf16[192,768]{1,0:T(8,128)(2,1)S(1)}, bf16[192,768]{1,0:T(8,128)(2,1)}, u32[]{:S(2)}) copy-start(bf16[192,768]{1,0:T(8,128)(2,1)} %refs_7_.1) | copy-start | bytes 884740
  5.4 1.0 %copy-start.2 = (bf16[192,768]{1,0:T(8,128)(2,1)S(1)}, bf16[192,768]{1,0:T(8,128)(2,1)}, u32[]{:S(2)}) copy-start(bf16[192,768]{1,0:T(8,128)(2,1)} %refs_8_.1) | copy-start | bytes 884740
  6.3 1.0 %copy-start.3 = (bf16[192,768]{1,0:T(8,128)(2,1)S(1)}, bf16[192,768]{1,0:T(8,128)(2,1)}, u32[]{:S(2)}) copy-start(bf16[192,768]{1,0:T(8,128)(2,1)} %refs_9_.1) | copy-start | bytes 884740
  7.3 1.0 %copy-start.4 = (bf16[192,768]{1,0:T(8,128)(2,1)S(1)}, bf16[192,768]{1,0:T(8,128)(2,1)}, u32[]{:S(2)}) copy-start(bf16[192,768]{1,0:T(8,128)(2,1)} %refs_10_.1) | copy-start | bytes 884740
  8.2 1.0 %copy-start.5 = (bf16[192,768]{1,0:T(8,128)(2,1)S(1)}, bf16[192,768]{1,0:T(8,128)(2,1)}, u32[]{:S(2)}) copy-start(bf16[192,768]{1,0:T(8,128)(2,1)} %refs_11_.1) | copy-start | bytes 884740
  9.2 0.9 copy-start.6
  10.1 0.9 copy-start.7
  11.0 0.9 copy-start.8
  11.9 0.9 copy-start.9
  12.7 0.7 copy-start.10
  13.4 0.7 copy-start.11
  14.1 0.7 copy-start.12

commit v2 on v1

--- a/solution.py
+++ b/solution.py
@@ -246,7 +246,7 @@
 
 
 def fits_fused(mesh):
-    return mesh.shape["tile"] == 8 and mesh.shape["row"] == 2
+    return (mesh.shape["tile"], mesh.shape["row"], mesh.shape["col"]) == (8, 2, 2)
 
 
 def contract_rows(first_op, second_op):
@@ -265,18 +265,18 @@
     count_ref,
     mask_ref,
     tok_hbm,
-    enc_gain_ref,
-    final_gain_ref,
-    slide_gain_ref,
-    wq_ref,
-    wk_ref,
-    wv_ref,
-    wo_ref,
-    wp_ref,
-    sq_ref,
-    sk_ref,
-    sv_ref,
-    so_ref,
+    enc_gain_hbm,
+    final_gain_hbm,
+    slide_gain_hbm,
+    wq_hbm,
+    wk_hbm,
+    wv_hbm,
+    wo_hbm,
+    wp_hbm,
+    sq_hbm,
+    sk_hbm,
+    sv_hbm,
+    so_hbm,
     grid_ref,
     branch_ref,
     cls,
@@ -306,6 +306,14 @@
     gains,
     live,
     slide_w,
+    wq_ref,
+    wk_ref,
+    wv_ref,
+    wo_ref,
+    wp_ref,
+    enc_gain_ref,
+    final_gain_ref,
+    slide_gain_ref,
     in_sem,
     send_sem,
     recv_sem,
@@ -318,7 +326,8 @@
     shard = width // tiles
     half = inner // 2
     heads = inner // HD
-    half_heads = heads // 2
+    third = inner // slots
+    third_heads = heads // slots
     bf, f32 = jnp.bfloat16, jnp.float32
     me = lax.axis_index("tile")
     my_row = lax.axis_index("row")
@@ -328,7 +337,36 @@
     first_in = pltpu.make_async_copy(tok_hbm.at[:, pl.ds(0, 16), :], cls, in_sem.at[0])
     first_in.start()
     whole_in = pltpu.make_async_copy(tok_hbm, tok, in_sem.at[1])
+    gain_ins = []
+    for place, (source, landing) in enumerate(
+        (
+            (enc_gain_hbm, enc_gain_ref),
+            (final_gain_hbm, final_gain_ref),
+            (slide_gain_hbm, slide_gain_ref),
+        )
+    ):
+        gain_ins.append(pltpu.make_async_copy(source, landing, in_sem.at[2 + place]))
+        gain_ins[-1].start()
+    weight_ins = []
+    for place, (source, landing) in enumerate(
+        ((wq_hbm, wq_ref), (wp_hbm, wp_ref), (wk_hbm, wk_ref), (wv_hbm, wv_ref), (wo_hbm, wo_ref))
+    ):
+        weight_ins.append(pltpu.make_async_copy(source, landing, in_sem.at[5 + place]))
+    wq_in, wp_in, wk_in, wv_in, wo_in = weight_ins
+    wq_in.start()
+    mine = my_row * 2 + my_col
+    own_pair = pl.ds(my_row * 2, 2)
+    for which, source in enumerate((sq_hbm, sk_hbm, sv_hbm, so_hbm)):
+
+        @pl.when(mine == which)
+        def bring(source=source):
+            pltpu.make_async_copy(source, slide_w.at[mine, me], in_sem.at[10]).start()
+
+    own_in = pltpu.make_async_copy(sq_hbm, slide_w.at[mine, me], in_sem.at[10])
+    wp_in.start()
     whole_in.start()
+    for copy in (wk_in, wv_in, wo_in):
+        copy.start()
 
     blank = jnp.where(
         lax.broadcasted_iota(jnp.int32, (8, halo.shape[2]), 1) == halo_lane(halo), FAR_BIAS, 0.0
@@ -362,15 +400,18 @@
     first_in.wait()
     raw = [cls[slot].astype(f32)[0:1] for slot in range(slots)]
     raw_rows = jnp.concatenate(raw, axis=0)
-    enc_gain = enc_gain_ref[...]
+    for copy in gain_ins:
+        copy.wait()
+    enc_gain = enc_gain_ref[...].reshape(1, width)
+    final_gain = final_gain_ref[...].reshape(1, width)
     class_normed = layer_norm(raw_rows, enc_gain, 1e-06).astype(bf).astype(f32)
     class_rows = jnp.concatenate(
-        [class_normed, raw_rows, jnp.zeros((8 - 2 * slots, width), f32)], axis=0
-    )
+        [class_normed] * 3 + [raw_rows, jnp.zeros((16 - 4 * slots, width), f32)], axis=0
+    ).astype(bf)
     for to in range(tiles):
         s1[to, :, :shard] = class_rows[:, to * shard : (to + 1) * shard]
         gains[to, :, :shard] = jnp.broadcast_to(
-            final_gain_ref[:, to * shard : (to + 1) * shard], (8, shard)
+            final_gain[:, to * shard : (to + 1) * shard], (8, shard)
         )
 
     pl.semaphore_wait(barrier, tiles - 1 + near_count)
@@ -401,22 +442,83 @@
 
     copies1 = send(0, s1, r1)
 
-    own_pair = pl.ds(my_row * 2, 2)
-    first_core = my_row == 0
-    slide_w[my_row * 2, me] = jnp.where(first_core, sq_ref[...], sv_ref[...])
-    slide_w[my_row * 2 + 1, me] = jnp.where(first_core, sk_ref[...], so_ref[...])
-    w_copies = []
-    for step in range(1, tiles):
-        copy = pltpu.make_async_remote_copy(
-            src_ref=slide_w.at[own_pair, me],
-            dst_ref=slide_w.at[own_pair, me],
-            send_sem=w_send.at[step],
-            recv_sem=w_recv.at[step],
-            device_id={"tile": lax.rem(me + step, tiles)},
+    own_in.wait()
+
+    def relay_copy(hop, side):
+        onward = 2 if side == 0 else -2
+        held = me - onward * hop
+        return pltpu.make_async_remote_copy(
+            src_ref=slide_w.at[mine, held],
+            dst_ref=slide_w.at[mine, held],
+            send_sem=w_send.at[side, hop],
+            recv_sem=w_recv.at[side, hop],
+            device_id={"tile": me + onward},
             device_id_type=MESH_ID,
         )
-        copy.start()
-        w_copies.append(copy)
+
+    def relay_inside(place):
+        return (place >= 0) & (place < tiles)
+
+    def relay_send(hop):
+        for side, onward in ((0, 2), (1, -2)):
+
+            @pl.when(relay_inside(me + onward) & relay_inside(me - onward * hop))
+            def go(side=side):
+                relay_copy(hop, side).start()
+
+    def relay_sent(hop):
+        for side, onward in ((0, 2), (1, -2)):
+
+            @pl.when(relay_inside(me + onward) & relay_inside(me - onward * hop))
+            def done(side=side):
+                relay_copy(hop, side).wait_send()
+
+    def relay_take(hop):
+        for side, onward in ((0, 2), (1, -2)):
+            held = me - onward * (hop + 1)
+
+            @pl.when(relay_inside(held))
+            def take(side=side, onward=onward, held=held):
+                pltpu.make_async_remote_copy(
+                    src_ref=slide_w.at[mine, held],
+                    dst_ref=slide_w.at[mine, held],
+                    send_sem=w_send.at[side, hop],
+                    recv_sem=w_recv.at[side, hop],
+                    device_id={"tile": me - onward},
+                    device_id_type=MESH_ID,
+                ).wait_recv()
+
+    side_y = lax.rem(me, 2)
+    lines = tiles // 2
+
+    def across(place, parity):
+        shard_at = place * 2 + parity
+        return pltpu.make_async_remote_copy(
+            src_ref=slide_w.at[mine, shard_at],
+            dst_ref=slide_w.at[mine, shard_at],
+            send_sem=w_send.at[2, place],
+            recv_sem=w_recv.at[2, place],
+            device_id={"tile": me + 1 - 2 * side_y},
+            device_id_type=MESH_ID,
+        )
+
+    over_x = pltpu.make_async_remote_copy(
+        src_ref=slide_w.at[mine],
+        dst_ref=slide_w.at[mine],
+        send_sem=w_send.at[3, 0],
+        recv_sem=w_recv.at[3, 0],
+        device_id={"col": 1 - my_col},
+        device_id_type=MESH_ID,
+    )
+    pair_copy = pltpu.make_async_remote_copy(
+        src_ref=slide_w.at[own_pair],
+        dst_ref=slide_w.at[own_pair],
+        send_sem=w_send.at[3, 1],
+        recv_sem=w_recv.at[3, 1],
+        device_id={"row": 1 - my_row},
+        device_id_type=MESH_ID,
+    )
+    relay_send(0)
 
     row64 = lax.broadcasted_iota(jnp.int32, (8 * tiles, 1), 0)
     in_block = lax.rem(row64, 8)
@@ -432,6 +534,7 @@
     whole_chunks = slots * per_tile
     whole_in.wait()
     my_gain = gains[me][:, :shard]
+    wp_in.wait()
     gain_high = my_gain.astype(bf)
     gain_low = (my_gain - gain_high.astype(f32)).astype(bf)
     sums = [
@@ -441,11 +544,10 @@
     ]
     low_rows = lax.broadcasted_iota(jnp.int32, (8, 1), 0) < 4
     sg[...] = jnp.where(low_rows, sums[0], sums[1])
-    copies_g = send(7, sg, rg)
-
-    col64 = lax.broadcasted_iota(jnp.int32, (8 * tiles, 8 * tiles), 1)
-    row_full = lax.broadcasted_iota(jnp.int32, (8 * tiles, 8 * tiles), 0)
-    place_low = jnp.zeros((8 * tiles, 8 * tiles), f32)
+
+    col64 = lax.broadcasted_iota(jnp.int32, (8 * tiles, 16 * tiles), 1)
+    row_full = lax.broadcasted_iota(jnp.int32, (8 * tiles, 16 * tiles), 0)
+    place_low = jnp.zeros((8 * tiles, 16 * tiles), f32)
     grid_cols = BLOCK * cols_n
     group = my_row * cols_n + my_col
     row_key = lax.div(row_full, 8) * 4 + lax.rem(row_full, 4)
@@ -459,56 +561,65 @@
             owner = lax.div(cell_row, jnp.int32(BLOCK * rows_n))
             spot = owner * 4 + lax.rem(cell_row, BLOCK) * BLOCK + lax.rem(cell_col, BLOCK)
             spot = jnp.where(slot < count, spot, -1)
-            hit = (row_key == spot) & (col64 == other * 8 + slot)
+            hit = (row_key == spot) & (col64 == other * 16 + slot)
             place_low = jnp.where(hit, 1.0, place_low)
-    place_high = jnp.concatenate([jnp.zeros((8 * tiles, slots), f32), place_low[:, :-slots]], axis=1)
+    placing = [
+        jnp.concatenate(
+            [jnp.zeros((8 * tiles, slots * turn), f32), place_low[:, : -slots * turn]], axis=1
+        ).astype(bf)
+        for turn in range(1, 4)
+    ]
     live_col = jnp.sum(place_low, axis=1, keepdims=True)
     live[...] = jnp.broadcast_to(live_col, (8 * tiles, 128)).reshape(tiles, 8, 128)
-    place_low = place_low.astype(bf)
-    place_high = place_high.astype(bf)
+    placing.insert(0, place_low.astype(bf))
 
     arrive(copies1)
-    shards1 = r1[...].reshape(8 * tiles, r1.shape[2])[:, :shard].astype(bf)
-    part_low = matmul(shards1, wq_ref[:, :half])
-    part_high = matmul(shards1, wq_ref[:, half:])
-    shifted = jnp.concatenate([part_high[-slots:], part_high[:-slots]], axis=0)
-    s2[...] = jnp.where(in_block < slots, part_low, shifted).reshape(s2.shape)
+    wq_in.wait()
+    shards1 = r1[...].reshape(16 * tiles, r1.shape[2])[:, :shard]
+    in_wide = lax.rem(lax.broadcasted_iota(jnp.int32, (16 * tiles, 1), 0), 16)
+    parts = [matmul(shards1, wq_ref[:, third * k : third * (k + 1)]) for k in range(3)]
+    packed_part = jnp.where(
+        in_wide < slots, parts[0], jnp.where(in_wide < 2 * slots, parts[1], parts[2])
+    )
+    s2[...] = packed_part.astype(bf).reshape(s2.shape)
     copies2 = send(1, s2, r2)
+    relay_take(0)
+    relay_send(1)
     lax.fori_loop(0, whole_chunks // 3, norm_chunk, 0)
     arrive(copies2)
-    s3[...] = jnp.sum(r2[...], axis=0).astype(bf).astype(f32)
+    s3[...] = jnp.sum(r2[...].astype(f32), axis=0).astype(bf)
     copies3 = send(2, s3, r3)
+    relay_take(1)
+    relay_send(2)
     lax.fori_loop(whole_chunks // 3, 2 * (whole_chunks // 3), norm_chunk, 0)
 
     wide_rows = 48 * tiles
-    exp_row = lax.broadcasted_iota(jnp.int32, (wide_rows, 8 * tiles), 0)
-    exp_col = lax.broadcasted_iota(jnp.int32, (wide_rows, 8 * tiles), 1)
+    exp_row = lax.broadcasted_iota(jnp.int32, (wide_rows, 16 * tiles), 0)
+    exp_col = lax.broadcasted_iota(jnp.int32, (wide_rows, 16 * tiles), 1)
     exp_in = lax.rem(exp_row, 48)
     exp_slot = lax.div(exp_in, heads)
     exp_head = lax.rem(exp_in, heads)
-    exp_base = lax.div(exp_row, 48) * 8 + exp_slot
-    real = exp_slot < slots
-    pick_low = (real & (exp_head < half_heads) & (exp_col == exp_base)).astype(f32).astype(bf)
-    pick_high = (
-        (real & (exp_head >= half_heads) & (exp_col == exp_base + slots)).astype(f32).astype(bf)
-    )
+    exp_turn = lax.div(exp_head, third_heads)
+    exp_base = lax.div(exp_row, 48) * 16 + exp_turn * slots + exp_slot
+    pick = ((exp_slot < slots) & (exp_col == exp_base)).astype(f32).astype(bf)
     head_of_row = lax.rem(
-        lax.rem(lax.broadcasted_iota(jnp.int32, (wide_rows, half), 0), 48), heads
-    )
-    head_of_col = lax.div(lax.broadcasted_iota(jnp.int32, (wide_rows, half), 1), HD)
-    own_low = head_of_row == head_of_col
-    own_high = head_of_row == head_of_col + half_heads
+        lax.rem(lax.broadcasted_iota(jnp.int32, (wide_rows, third), 0), 48), heads
+    )
+    head_of_col = lax.div(lax.broadcasted_iota(jnp.int32, (wide_rows, third), 1), HD)
+    own = [head_of_row == head_of_col + turn * third_heads for turn in range(3)]
     arrive(copies3)
-    queries = r3[...].reshape(8 * tiles, half).astype(bf)
-    query_low = jnp.where(own_low, matmul(pick_low, queries), 0.0).astype(bf)
-    query_high = jnp.where(own_high, matmul(pick_high, queries), 0.0).astype(bf)
-    folded = contract_rows(query_low, wk_ref[:, :half]) + contract_rows(
-        query_high, wk_ref[:, half:]
-    )
+    wk_in.wait()
+    queries = matmul(pick, r3[...].reshape(16 * tiles, third))
+    query_wide = jnp.concatenate([jnp.where(at, queries, 0.0) for at in own], axis=1).astype(bf)
+    folded = contract_rows(query_wide, wk_ref[...])
     s4[:, :, :shard] = folded.astype(bf).reshape(tiles, 48, shard)
     copies4 = send(3, s4, r4)
     lax.fori_loop(2 * (whole_chunks // 3), whole_chunks, norm_chunk, 0)
     arrive(copies4)
+    copies_g = send(7, sg, rg)
+    relay_take(2)
+    for place in range(lines):
+        across(place, side_y).start()
 
     for other in range(tiles):
         wide[:, other * shard : (other + 1) * shard] = r4[other, :, :shard]
@@ -525,43 +636,33 @@
     for to in range(tiles):
         s5[to, :, :shard] = mixed[:, to * shard : (to + 1) * shard]
     copies5 = send(4, s5, r5)
+    for place in range(lines):
+        across(place, 1 - side_y).wait_recv()
+    over_x.start()
     arrive(copies5)
+    wv_in.wait()
 
     mixes = r5[...].reshape(wide_rows, r5.shape[2])[:, :shard]
-    value_low = jnp.where(own_low, matmul(mixes, wv_ref[:, :half]), 0.0).astype(bf)
-    value_high = jnp.where(own_high, matmul(mixes, wv_ref[:, half:]), 0.0).astype(bf)
-    columns0 = (((0,), (0,)), ((), ()))
+    valued = jnp.zeros((wide_rows, third), f32)
+    for turn in range(3):
+        columns = wv_ref[:, third * turn : third * (turn + 1)]
+        valued = jnp.where(own[turn], matmul(mixes, columns), valued)
     gathered = lax.dot_general(
-        pick_low, value_low, columns0, preferred_element_type=f32
-    ) + lax.dot_general(pick_high, value_high, columns0, preferred_element_type=f32)
+        pick, valued.astype(bf), (((0,), (0,)), ((), ())), preferred_element_type=f32
+    ).astype(bf)
     s6[...] = gathered.reshape(s6.shape)
     copies6 = send(5, s6, r6)
     arrive(copies6)
-    s7[...] = jnp.sum(r6[...], axis=0).astype(bf).astype(f32)
+    s7[...] = jnp.sum(r6[...].astype(f32), axis=0).astype(bf)
     copies7 = send(6, s7, r7)
-    raw_cells = matmul(place_high, shards1)
-
-    for copy in w_copies:
-        copy.wait_recv()
-    pair_copy = pltpu.make_async_remote_copy(
-        src_ref=slide_w.at[own_pair],
-        dst_ref=slide_w.at[own_pair],
-        send_sem=w_send.at[0],
-        recv_sem=w_recv.at[0],
-        device_id={"row": 1 - my_row},
-        device_id_type=MESH_ID,
-    )
-    pair_copy.start()
+    raw_cells = matmul(placing[3], shards1)
+
     arrive(copies7)
-
-    mix_rows = r7[...].reshape(8 * tiles, half).astype(bf)
-    cell_low = matmul(place_low, mix_rows).astype(bf)
-    cell_high = matmul(place_high, mix_rows).astype(bf)
-    carried = (
-        raw_cells
-        + contract_rows(cell_low, wo_ref[:, :half])
-        + contract_rows(cell_high, wo_ref[:, half:])
-    )
+    wo_in.wait()
+
+    mix_rows = r7[...].reshape(16 * tiles, third)
+    cell_mix = jnp.concatenate([matmul(placing[k], mix_rows) for k in range(3)], axis=1)
+    carried = raw_cells + contract_rows(cell_mix.astype(bf), wo_ref[...])
     part_mean = jnp.mean(carried, axis=1, keepdims=True)
     centered = carried - part_mean
     part_square = jnp.sum(centered * centered, axis=1, keepdims=True)
@@ -573,6 +674,8 @@
     lane = lax.broadcasted_iota(jnp.int32, (8 * tiles, 128), 1)
     s9[:, :, half:] = jnp.where(lane == 0, part_mean, part_square).reshape(tiles, 8, 128)
     copies9 = send(8, s9, r9)
+    over_x.wait_recv()
+    pair_copy.start()
     arrive(copies_g)
     arrive(copies9)
 
@@ -592,9 +695,9 @@
     grid_ref[1] = cells[2:4].astype(bf)
 
     pair_copy.wait_recv()
-    inner_s = so_ref.shape[1]
+    inner_s = slide_w.shape[3]
     slide_rows = jnp.concatenate([cells, cells], axis=0)
-    slide_in = layer_norm(slide_rows, slide_gain_ref[...], 1e-05).astype(bf)
+    slide_in = layer_norm(slide_rows, slide_gain_ref[...].reshape(1, -1), 1e-05).astype(bf)
 
     def slide_full(which):
         return slide_w[which].reshape(-1, inner_s)
@@ -677,8 +780,10 @@
     branch_ref[0] = branch[0:2]
     branch_ref[1] = branch[2:4]
 
-    for copy in started + w_copies + [pair_copy]:
+    for copy in started + [across(place, side_y) for place in range(lines)] + [over_x, pair_copy]:
         copy.wait_send()
+    for hop in range(3):
+        relay_sent(hop)
     for (inside, target), copy in zip(beside, halo_copies):
 
         @pl.when(inside)
@@ -721,7 +826,9 @@
     bf, f32 = jnp.bfloat16, jnp.float32
     vmem = pl.BlockSpec(memory_space=pltpu.VMEM)
     smem = pl.BlockSpec(memory_space=pltpu.SMEM)
-    slab = pltpu.VMEM((tiles, 8, 256), f32)
+    slab = pltpu.VMEM((tiles, 16, 256), bf)
+    thirds = pltpu.VMEM((tiles, 16, inner // 3), bf)
+    one_third = pltpu.VMEM((16, inner // 3), bf)
     packed = pltpu.VMEM((tiles, 8, half), f32)
     one_packed = pltpu.VMEM((8, half), f32)
     heads_slab = pltpu.VMEM((tiles, 48, 256), bf)
@@ -736,7 +843,7 @@
             jax.ShapeDtypeStruct((BLOCK, BLOCK, model), bf),
             jax.ShapeDtypeStruct((BLOCK, BLOCK, model), f32),
         ),
-        in_specs=[smem] * 3 + [pl.BlockSpec(memory_space=pl.ANY)] + [vmem] * 12,
+        in_specs=[smem] * 3 + [pl.BlockSpec(memory_space=pl.ANY)] * 13,
         out_specs=(vmem, vmem),
         scratch_shapes=[
             pltpu.VMEM((slots, 16, width), bf),
@@ -744,18 +851,18 @@
             pltpu.VMEM((slots * patch, width), bf),
             slab,
             slab,
-            packed,
-            packed,
-            one_packed,
-            packed,
+            thirds,
+            thirds,
+            one_third,
+            thirds,
             heads_slab,
             heads_slab,
             heads_slab,
             heads_slab,
-            packed,
-            packed,
-            one_packed,
-            packed,
+            thirds,
+            thirds,
+            one_third,
+            thirds,
             stat_slab,
             stat_slab,
             one_packed,
@@ -763,28 +870,36 @@
             pltpu.VMEM((8, inner_s + 128), f32),
             pltpu.VMEM((9, 8, inner_s + 128), f32),
             pltpu.VMEM((48, width), bf),
-            slab,
+            pltpu.VMEM((tiles, 8, 256), f32),
             pltpu.VMEM((tiles, 8, 128), f32),
             pltpu.VMEM((4, tiles, s_query.shape[0], inner_s), bf),
-            pltpu.SemaphoreType.DMA((2,)),
+            pltpu.VMEM(w_query.shape, bf),
+            pltpu.VMEM(w_key.shape, bf),
+            pltpu.VMEM(w_value.shape, bf),
+            pltpu.VMEM(w_out_t.shape, bf),
+            pltpu.VMEM(w_proj.shape, bf),
+            pltpu.VMEM((width,), f32),
+            pltpu.VMEM((width,), f32),
+            pltpu.VMEM((model,), f32),
+            pltpu.SemaphoreType.DMA((12,)),
             pltpu.SemaphoreType.DMA((PHASES + 1, tiles)),
             pltpu.SemaphoreType.DMA((PHASES + 1, tiles)),
-            pltpu.SemaphoreType.DMA((tiles,)),
-            pltpu.SemaphoreType.DMA((tiles,)),
+            pltpu.SemaphoreType.DMA((4, tiles)),
+            pltpu.SemaphoreType.DMA((4, tiles)),
             pltpu.SemaphoreType.DMA((8,)),
             pltpu.SemaphoreType.DMA((8,)),
         ],
         compiler_params=pltpu.CompilerParams(
-            collective_id=0, has_side_effects=True, vmem_limit_bytes=48 * 1024 * 1024
+            collective_id=0, has_side_effects=True, vmem_limit_bytes=60 * 1024 * 1024
         ),
     )(
         tile_cell,
         tile_count,
         block_mask,
         tile_tokens,
-        enc_gain.reshape(1, width),
-        final_gain.reshape(1, width),
-        slide_gain.reshape(1, model),
+        enc_gain,
+        final_gain,
+        slide_gain,
         w_query,
         w_key,
         w_value,

time: 94.6 us -> 59.1 us (0.62)
  Pallas kernels: 78 us -> 55.5 us
  local copies, waits for them, and re-layouts: 15.3 us -> 2.6 us
    pallas_call x1, Pallas kernels: 78 us -> 55.5 us  [fused(): pl.pallas_call(kernel, out_shape=(jax.ShapeDtypeStruct((BLOCK, BLOCK, mod...]
    unnamed x28 -> x2, local copies, waits for them, and re-layouts: 13.2 us -> 2.6 us
    reshape x3 -> x0, local copies, waits for them, and re-layouts: 2.09 us -> none  [the longest x1 0.7 us: fused(): enc_gain.reshape(1, width)]
where the time goes in v2:
time: 59.1 us; the launch traced here: 58.8 us
  Pallas kernels  55.5 us (94%)
  local copies, waits for them, and re-layouts  2.6 us (4%)
  between operations  0.65 us (1%)
    pallas_call x1, Pallas kernels, fused(): pl.pallas_call(kernel, out_shape=(jax.ShapeDtypeStruct((BLOCK, BLOCK, mod...  55.5 us
    unnamed x2, local copies, waits for them, and re-layouts  2.6 us

profile of v2, /device:TPU:1, one launch (start us, length us, event | category | flops | bytes accessed | tf_op | source)
XLA Modules:
  0.0 58.8 jit_solution(13077653976712506820)
XLA Ops:
  0.6 55.5 %shard_map.167 = (bf16[2,2,768]{2,1,0:T(2,128)(2,1)}, f32[2,2,768]{2,1,0:T(2,128)}) custom-call(s32[96]{0:T(128)} %refs_0_.1, s32[32]{0:T(128)} %refs_1_.1, s32[1,1,8]{2,1,0:T(1,128)} %refs_2_.1, bf16[3,256,1536]{2,1,0:T(8,128)(2,1)} %refs_3_.1, f32[1536]{0:T(1024)} %refs_4_.1, f32[1536]{0:T(1024)} %refs_5_.1, f32[768]{0:T(1024)} %refs_6_.1, ...), custom_call_target="tpu_custom_call" | custom-call | tf_op jit(solution)/shard_map/pallas_call | solution.py:840
  56.2 1.3 %copy.20 = bf16[2,2,768]{2,1,0:T(2,128)(2,1)} copy(bf16[2,2,768]{2,1,0:T(2,128)(2,1)} %get-tuple-element.4) | data formatting | bytes 12288
  57.5 1.3 %copy.21 = f32[2,2,768]{2,1,0:T(2,128)} copy(f32[2,2,768]{2,1,0:T(2,128)} %get-tuple-element.5) | data formatting | bytes 24576

commit v3 on v2

--- a/solution.py
+++ b/solution.py
@@ -290,10 +290,6 @@
     r3,
     s4,
     r4,
-    s5,
-    r5,
-    s6,
-    r6,
     s7,
     r7,
     s9,
@@ -321,6 +317,8 @@
     w_recv,
     halo_send,
     halo_recv,
+    v_send,
+    v_recv,
 ):
     tiles, rows_n, cols_n, slots, patch, width, inner = sizes
     shard = width // tiles
@@ -348,12 +346,15 @@
         gain_ins.append(pltpu.make_async_copy(source, landing, in_sem.at[2 + place]))
         gain_ins[-1].start()
     weight_ins = []
+    cut = shard // 2
+    wv_own = wv_hbm.at[pl.ds(pl.multiple_of(my_row * cut, cut), cut), :]
     for place, (source, landing) in enumerate(
-        ((wq_hbm, wq_ref), (wp_hbm, wp_ref), (wk_hbm, wk_ref), (wv_hbm, wv_ref), (wo_hbm, wo_ref))
+        ((wq_hbm, wq_ref), (wp_hbm, wp_ref), (wk_hbm, wk_ref), (wv_own, wv_ref.at[me, my_row]), (wo_hbm, wo_ref))
     ):
         weight_ins.append(pltpu.make_async_copy(source, landing, in_sem.at[5 + place]))
     wq_in, wp_in, wk_in, wv_in, wo_in = weight_ins
     wq_in.start()
+    wv_in.start()
     mine = my_row * 2 + my_col
     own_pair = pl.ds(my_row * 2, 2)
     for which, source in enumerate((sq_hbm, sk_hbm, sv_hbm, so_hbm)):
@@ -365,7 +366,7 @@
     own_in = pltpu.make_async_copy(sq_hbm, slide_w.at[mine, me], in_sem.at[10])
     wp_in.start()
     whole_in.start()
-    for copy in (wk_in, wv_in, wo_in):
+    for copy in (wk_in, wo_in):
         copy.start()
 
     blank = jnp.where(
@@ -487,8 +488,56 @@
                     device_id={"tile": me - onward},
                     device_id_type=MESH_ID,
                 ).wait_recv()
+                onward_slide(held)
 
     side_y = lax.rem(me, 2)
+
+    def value_copy(target, held, way, hop):
+        return pltpu.make_async_remote_copy(
+            src_ref=wv_ref.at[held, my_row],
+            dst_ref=wv_ref.at[held, my_row],
+            send_sem=v_send.at[way, hop],
+            recv_sem=v_recv.at[way, hop],
+            device_id={"tile": target},
+            device_id_type=MESH_ID,
+        )
+
+    def value_line(hop, method):
+        for side, onward in ((0, 2), (1, -2)):
+
+            @pl.when(relay_inside(me + onward) & relay_inside(me - onward * hop))
+            def go(side=side, onward=onward):
+                getattr(value_copy(me + onward, me - onward * hop, side, hop), method)()
+
+    def value_take(hop):
+        for side, onward in ((0, 2), (1, -2)):
+
+            @pl.when(relay_inside(me - onward * (hop + 1)))
+            def go(side=side, onward=onward):
+                held = me - onward * (hop + 1)
+                value_copy(me - onward, held, side, hop).wait_recv()
+                value_across(held, side_y).start()
+
+    def value_across(held, parity):
+        place = lax.div(held, 2)
+        return value_copy(me + 1 - 2 * side_y, place * 2 + parity, 2, place)
+
+    def value_step(hop):
+        value_take(hop)
+        if hop < 2:
+            value_line(hop + 1, "start")
+
+    value_pair = pltpu.make_async_remote_copy(
+        src_ref=wv_ref.at[:, my_row],
+        dst_ref=wv_ref.at[:, my_row],
+        send_sem=v_send.at[3, 0],
+        recv_sem=v_recv.at[3, 0],
+        device_id={"row": 1 - my_row},
+        device_id_type=MESH_ID,
+    )
+    wv_in.wait()
+    value_line(0, "start")
+    value_across(me, side_y).start()
     lines = tiles // 2
 
     def across(place, parity):
@@ -502,23 +551,30 @@
             device_id_type=MESH_ID,
         )
 
-    over_x = pltpu.make_async_remote_copy(
-        src_ref=slide_w.at[mine],
-        dst_ref=slide_w.at[mine],
-        send_sem=w_send.at[3, 0],
-        recv_sem=w_recv.at[3, 0],
-        device_id={"col": 1 - my_col},
-        device_id_type=MESH_ID,
-    )
+    def over_x(shard_at, owned):
+        return pltpu.make_async_remote_copy(
+            src_ref=slide_w.at[owned, shard_at],
+            dst_ref=slide_w.at[owned, shard_at],
+            send_sem=w_send.at[3, shard_at],
+            recv_sem=w_recv.at[3, shard_at],
+            device_id={"col": 1 - my_col},
+            device_id_type=MESH_ID,
+        )
+
+    def onward_slide(shard_at):
+        across(lax.div(shard_at, 2), side_y).start()
+        over_x(shard_at, mine).start()
+
     pair_copy = pltpu.make_async_remote_copy(
         src_ref=slide_w.at[own_pair],
         dst_ref=slide_w.at[own_pair],
-        send_sem=w_send.at[3, 1],
-        recv_sem=w_recv.at[3, 1],
+        send_sem=w_send.at[4, 0],
+        recv_sem=w_recv.at[4, 0],
         device_id={"row": 1 - my_row},
         device_id_type=MESH_ID,
     )
     relay_send(0)
+    onward_slide(me)
 
     row64 = lax.broadcasted_iota(jnp.int32, (8 * tiles, 1), 0)
     in_block = lax.rem(row64, 8)
@@ -532,7 +588,6 @@
 
     per_tile = patch // 32
     whole_chunks = slots * per_tile
-    whole_in.wait()
     my_gain = gains[me][:, :shard]
     wp_in.wait()
     gain_high = my_gain.astype(bf)
@@ -544,7 +599,85 @@
     ]
     low_rows = lax.broadcasted_iota(jnp.int32, (8, 1), 0) < 4
     sg[...] = jnp.where(low_rows, sums[0], sums[1])
-
+    copies_g = send(7, sg, rg)
+
+    arrive(copies1)
+    wq_in.wait()
+    shards1 = r1[...].reshape(16 * tiles, r1.shape[2])[:, :shard]
+    in_wide = lax.rem(lax.broadcasted_iota(jnp.int32, (16 * tiles, 1), 0), 16)
+    parts = [matmul(shards1, wq_ref[:, third * k : third * (k + 1)]) for k in range(3)]
+    packed_part = jnp.where(
+        in_wide < slots, parts[0], jnp.where(in_wide < 2 * slots, parts[1], parts[2])
+    )
+    s2[...] = packed_part.astype(bf).reshape(s2.shape)
+    copies2 = send(1, s2, r2)
+    value_step(0)
+    relay_take(0)
+    relay_send(1)
+    whole_in.wait()
+    lax.fori_loop(0, whole_chunks // 3, norm_chunk, 0)
+    arrive(copies2)
+    s3[...] = jnp.sum(r2[...].astype(f32), axis=0).astype(bf)
+    copies3 = send(2, s3, r3)
+    value_step(1)
+    relay_take(1)
+    relay_send(2)
+    lax.fori_loop(whole_chunks // 3, 2 * (whole_chunks // 3), norm_chunk, 0)
+
+    wide_rows = 48 * tiles
+    exp_row = lax.broadcasted_iota(jnp.int32, (wide_rows, 16 * tiles), 0)
+    exp_col = lax.broadcasted_iota(jnp.int32, (wide_rows, 16 * tiles), 1)
+    exp_in = lax.rem(exp_row, 48)
+    exp_slot = lax.div(exp_in, heads)
+    exp_head = lax.rem(exp_in, heads)
+    exp_turn = lax.div(exp_head, third_heads)
+    exp_base = lax.div(exp_row, 48) * 16 + exp_turn * slots + exp_slot
+    pick = ((exp_slot < slots) & (exp_col == exp_base)).astype(f32).astype(bf)
+    head_of_row = lax.rem(
+        lax.rem(lax.broadcasted_iota(jnp.int32, (wide_rows, third), 0), 48), heads
+    )
+    head_of_col = lax.div(lax.broadcasted_iota(jnp.int32, (wide_rows, third), 1), HD)
+    own = [head_of_row == head_of_col + turn * third_heads for turn in range(3)]
+    arrive(copies3)
+    wk_in.wait()
+    queries = matmul(pick, r3[...].reshape(16 * tiles, third))
+    query_wide = jnp.concatenate([jnp.where(at, queries, 0.0) for at in own], axis=1).astype(bf)
+    folded = contract_rows(query_wide, wk_ref[...])
+    s4[:, :, :shard] = folded.astype(bf).reshape(tiles, 48, shard)
+    copies4 = send(3, s4, r4)
+    value_step(2)
+    relay_take(2)
+    lax.fori_loop(2 * (whole_chunks // 3), whole_chunks, norm_chunk, 0)
+    arrive(copies4)
+    for place in range(lines):
+        value_across(jnp.int32(2 * place), 1 - side_y).wait_recv()
+    value_pair.start()
+    for place in range(lines):
+        across(place, 1 - side_y).wait_recv()
+        over_x(place * 2 + 1 - side_y, mine).start()
+
+    for other in range(tiles):
+        wide[:, other * shard : (other + 1) * shard] = r4[other, :, :shard]
+    tokens = normed[...]
+    scores = contract_rows(wide[...], tokens) / math.sqrt(HD)
+    score_slot = lax.div(lax.broadcasted_iota(jnp.int32, scores.shape, 0), heads)
+    score_tile = lax.div(lax.broadcasted_iota(jnp.int32, scores.shape, 1), patch)
+    same = score_slot == score_tile
+    peak = jnp.max(jnp.where(same, scores, -1e30), axis=1, keepdims=True)
+    grown = jnp.where(same, jnp.exp(jnp.minimum(scores - peak, 0.0)), 0.0)
+    total = jnp.sum(grown, axis=1, keepdims=True)
+    probs = (grown / jnp.where(total > 0.0, total, 1.0)).astype(bf)
+    mixed = matmul(probs, tokens).astype(bf)
+    value_pair.wait_recv()
+    all_values = matmul(mixed, wv_ref[...].reshape(width, inner))
+    valued = jnp.zeros((48, third), f32)
+    for turn in range(3):
+        columns = all_values[:, third * turn : third * (turn + 1)]
+        valued = jnp.where(own[turn][:48], columns, valued)
+    s7[...] = lax.dot_general(
+        pick[:48, :16], valued.astype(bf), (((0,), (0,)), ((), ())), preferred_element_type=f32
+    ).astype(bf)
+    copies7 = send(6, s7, r7)
     col64 = lax.broadcasted_iota(jnp.int32, (8 * tiles, 16 * tiles), 1)
     row_full = lax.broadcasted_iota(jnp.int32, (8 * tiles, 16 * tiles), 0)
     place_low = jnp.zeros((8 * tiles, 16 * tiles), f32)
@@ -572,89 +705,6 @@
     live_col = jnp.sum(place_low, axis=1, keepdims=True)
     live[...] = jnp.broadcast_to(live_col, (8 * tiles, 128)).reshape(tiles, 8, 128)
     placing.insert(0, place_low.astype(bf))
-
-    arrive(copies1)
-    wq_in.wait()
-    shards1 = r1[...].reshape(16 * tiles, r1.shape[2])[:, :shard]
-    in_wide = lax.rem(lax.broadcasted_iota(jnp.int32, (16 * tiles, 1), 0), 16)
-    parts = [matmul(shards1, wq_ref[:, third * k : third * (k + 1)]) for k in range(3)]
-    packed_part = jnp.where(
-        in_wide < slots, parts[0], jnp.where(in_wide < 2 * slots, parts[1], parts[2])
-    )
-    s2[...] = packed_part.astype(bf).reshape(s2.shape)
-    copies2 = send(1, s2, r2)
-    relay_take(0)
-    relay_send(1)
-    lax.fori_loop(0, whole_chunks // 3, norm_chunk, 0)
-    arrive(copies2)
-    s3[...] = jnp.sum(r2[...].astype(f32), axis=0).astype(bf)
-    copies3 = send(2, s3, r3)
-    relay_take(1)
-    relay_send(2)
-    lax.fori_loop(whole_chunks // 3, 2 * (whole_chunks // 3), norm_chunk, 0)
-
-    wide_rows = 48 * tiles
-    exp_row = lax.broadcasted_iota(jnp.int32, (wide_rows, 16 * tiles), 0)
-    exp_col = lax.broadcasted_iota(jnp.int32, (wide_rows, 16 * tiles), 1)
-    exp_in = lax.rem(exp_row, 48)
-    exp_slot = lax.div(exp_in, heads)
-    exp_head = lax.rem(exp_in, heads)
-    exp_turn = lax.div(exp_head, third_heads)
-    exp_base = lax.div(exp_row, 48) * 16 + exp_turn * slots + exp_slot
-    pick = ((exp_slot < slots) & (exp_col == exp_base)).astype(f32).astype(bf)
-    head_of_row = lax.rem(
-        lax.rem(lax.broadcasted_iota(jnp.int32, (wide_rows, third), 0), 48), heads
-    )
-    head_of_col = lax.div(lax.broadcasted_iota(jnp.int32, (wide_rows, third), 1), HD)
-    own = [head_of_row == head_of_col + turn * third_heads for turn in range(3)]
-    arrive(copies3)
-    wk_in.wait()
-    queries = matmul(pick, r3[...].reshape(16 * tiles, third))
-    query_wide = jnp.concatenate([jnp.where(at, queries, 0.0) for at in own], axis=1).astype(bf)
-    folded = contract_rows(query_wide, wk_ref[...])
-    s4[:, :, :shard] = folded.astype(bf).reshape(tiles, 48, shard)
-    copies4 = send(3, s4, r4)
-    lax.fori_loop(2 * (whole_chunks // 3), whole_chunks, norm_chunk, 0)
-    arrive(copies4)
-    copies_g = send(7, sg, rg)
-    relay_take(2)
-    for place in range(lines):
-        across(place, side_y).start()
-
-    for other in range(tiles):
-        wide[:, other * shard : (other + 1) * shard] = r4[other, :, :shard]
-    tokens = normed[...]
-    scores = contract_rows(wide[...], tokens) / math.sqrt(HD)
-    score_slot = lax.div(lax.broadcasted_iota(jnp.int32, scores.shape, 0), heads)
-    score_tile = lax.div(lax.broadcasted_iota(jnp.int32, scores.shape, 1), patch)
-    same = score_slot == score_tile
-    peak = jnp.max(jnp.where(same, scores, -1e30), axis=1, keepdims=True)
-    grown = jnp.where(same, jnp.exp(jnp.minimum(scores - peak, 0.0)), 0.0)
-    total = jnp.sum(grown, axis=1, keepdims=True)
-    probs = (grown / jnp.where(total > 0.0, total, 1.0)).astype(bf)
-    mixed = matmul(probs, tokens).astype(bf)
-    for to in range(tiles):
-        s5[to, :, :shard] = mixed[:, to * shard : (to + 1) * shard]
-    copies5 = send(4, s5, r5)
-    for place in range(lines):
-        across(place, 1 - side_y).wait_recv()
-    over_x.start()
-    arrive(copies5)
-    wv_in.wait()
-
-    mixes = r5[...].reshape(wide_rows, r5.shape[2])[:, :shard]
-    valued = jnp.zeros((wide_rows, third), f32)
-    for turn in range(3):
-        columns = wv_ref[:, third * turn : third * (turn + 1)]
-        valued = jnp.where(own[turn], matmul(mixes, columns), valued)
-    gathered = lax.dot_general(
-        pick, valued.astype(bf), (((0,), (0,)), ((), ())), preferred_element_type=f32
-    ).astype(bf)
-    s6[...] = gathered.reshape(s6.shape)
-    copies6 = send(5, s6, r6)
-    arrive(copies6)
-    s7[...] = jnp.sum(r6[...].astype(f32), axis=0).astype(bf)
-    copies7 = send(6, s7, r7)
     raw_cells = matmul(placing[3], shards1)
 
     arrive(copies7)
@@ -674,7 +724,8 @@
     lane = lax.broadcasted_iota(jnp.int32, (8 * tiles, 128), 1)
     s9[:, :, half:] = jnp.where(lane == 0, part_mean, part_square).reshape(tiles, 8, 128)
     copies9 = send(8, s9, r9)
-    over_x.wait_recv()
+    for shard_at in range(tiles):
+        over_x(shard_at, my_row * 2 + 1 - my_col).wait_recv()
     pair_copy.start()
     arrive(copies_g)
     arrive(copies9)
@@ -780,10 +831,16 @@
     branch_ref[0] = branch[0:2]
     branch_ref[1] = branch[2:4]
 
-    for copy in started + [across(place, side_y) for place in range(lines)] + [over_x, pair_copy]:
+    for copy in started + [across(place, side_y) for place in range(lines)] + [pair_copy]:
         copy.wait_send()
+    value_pair.wait_send()
+    for shard_at in range(tiles):
+        over_x(shard_at, mine).wait_send()
+    for place in range(lines):
+        value_across(jnp.int32(2 * place), side_y).wait_send()
     for hop in range(3):
         relay_sent(hop)
+        value_line(hop, "wait_send")
     for (inside, target), copy in zip(beside, halo_copies):
 
         @pl.when(inside)
@@ -857,10 +914,6 @@
             thirds,
             heads_slab,
             heads_slab,
-            heads_slab,
-            heads_slab,
-            thirds,
-            thirds,
             one_third,
             thirds,
             stat_slab,
@@ -875,7 +928,7 @@
             pltpu.VMEM((4, tiles, s_query.shape[0], inner_s), bf),
             pltpu.VMEM(w_query.shape, bf),
             pltpu.VMEM(w_key.shape, bf),
-            pltpu.VMEM(w_value.shape, bf),
+            pltpu.VMEM((tiles, 2, w_value.shape[0] // 2, inner), bf),
             pltpu.VMEM(w_out_t.shape, bf),
             pltpu.VMEM(w_proj.shape, bf),
             pltpu.VMEM((width,), f32),
@@ -884,10 +937,12 @@
             pltpu.SemaphoreType.DMA((12,)),
             pltpu.SemaphoreType.DMA((PHASES + 1, tiles)),
             pltpu.SemaphoreType.DMA((PHASES + 1, tiles)),
-            pltpu.SemaphoreType.DMA((4, tiles)),
-            pltpu.SemaphoreType.DMA((4, tiles)),
+            pltpu.SemaphoreType.DMA((5, tiles)),
+            pltpu.SemaphoreType.DMA((5, tiles)),
             pltpu.SemaphoreType.DMA((8,)),
             pltpu.SemaphoreType.DMA((8,)),
+            pltpu.SemaphoreType.DMA((4, 4)),
+            pltpu.SemaphoreType.DMA((4, 4)),
         ],
         compiler_params=pltpu.CompilerParams(
             collective_id=0, has_side_effects=True, vmem_limit_bytes=60 * 1024 * 1024

time: 59.1 us -> 56.7 us (0.959)
  Pallas kernels: 55.5 us -> 53.2 us
    pallas_call x1, Pallas kernels: 55.5 us -> 53.2 us  [fused(): pl.pallas_call(kernel, out_shape=(jax.ShapeDtypeStruct((BLOCK, BLOCK, mod...]
where the time goes in v3:
time: 56.7 us; the launch traced here: 56.4 us
  Pallas kernels  53.2 us (94%)
  local copies, waits for them, and re-layouts  2.6 us (5%)
  between operations  0.65 us (1%)
    pallas_call x1, Pallas kernels, fused(): pl.pallas_call(kernel, out_shape=(jax.ShapeDtypeStruct((BLOCK, BLOCK, mod...  53.2 us
    unnamed x2, local copies, waits for them, and re-layouts  2.6 us

profile of v3, /device:TPU:1, one launch (start us, length us, event | category | flops | bytes accessed | tf_op | source)
XLA Modules:
  0.0 56.4 jit_solution(13704099023829917282)
XLA Ops:
  0.6 53.2 %shard_map.167 = (bf16[2,2,768]{2,1,0:T(2,128)(2,1)}, f32[2,2,768]{2,1,0:T(2,128)}) custom-call(s32[96]{0:T(128)} %refs_0_.1, s32[32]{0:T(128)} %refs_1_.1, s32[1,1,8]{2,1,0:T(1,128)} %refs_2_.1, bf16[3,256,1536]{2,1,0:T(8,128)(2,1)} %refs_3_.1, f32[1536]{0:T(1024)} %refs_4_.1, f32[1536]{0:T(1024)} %refs_5_.1, f32[768]{0:T(1024)} %refs_6_.1, ...), custom_call_target="tpu_custom_call" | custom-call | tf_op jit(solution)/shard_map/pallas_call | solution.py:897
  53.8 1.3 %copy.20 = bf16[2,2,768]{2,1,0:T(2,128)(2,1)} copy(bf16[2,2,768]{2,1,0:T(2,128)(2,1)} %get-tuple-element.4) | data formatting | bytes 12288
  55.1 1.3 %copy.21 = f32[2,2,768]{2,1,0:T(2,128)} copy(f32[2,2,768]{2,1,0:T(2,128)} %get-tuple-element.5) | data formatting | bytes 24576
